TPU v7x, 32 devices: a whole 2x2x4 slice. The times are simulated.
32 devices in a mesh: lat: 8 (over z, y), lon: 2 (over x), comp: 2 (over core).
Axes of the slice: x: 2, y: 2, z: 4, core: 2. Of those that a mesh axis runs over, the one named last changes fastest.
Arguments:
- atm_state: bfloat16 [2, 16, 512, 384], P(None, 'lat', ('lon', 'comp')), may hold values from -6 to 6
- ocean_prev: bfloat16 [2, 16, 512, 128], P(None, 'lat', ('lon', 'comp')), may hold values from -6 to 6
- land_sea: int32 [16, 512], P('lat', ('lon', 'comp')), may hold values 0 or 1
- window_ids: int32 [16, 512], P('lat', ('lon', 'comp')), may hold values from 0 to 511, as said below
- conv_atm: float32 [2, 3, 3, 384], replicated, may hold values from -2 to 2
- attn_gain: float32 [2, 384], replicated, may hold values from 0.5 to 2
- qkv_matrix: bfloat16 [2, 384, 1152], replicated, may hold values from -0.3125 to 0.3125
- attn_scales: float32 [2, 6], replicated, may hold values from 4 to 32
- out_matrix: bfloat16 [2, 384, 384], replicated, may hold values from -0.3125 to 0.3125
- mlp_gain: float32 [2, 384], replicated, may hold values from 0.5 to 2
- member_in: float32 [2, 2, 384], replicated, may hold values from 0.5 to 2
- member_out: float32 [2, 2, 1536], replicated, may hold values from 0.5 to 2
- up_matrix: bfloat16 [2, 384, 1536], replicated, may hold values from -0.3125 to 0.3125
- down_matrix: bfloat16 [2, 1536, 384], replicated, may hold values from -0.15625 to 0.15625
- flux_matrix: bfloat16 [384, 128], replicated, may hold values from -0.3125 to 0.3125
- conv_ocean: float32 [3, 3, 3, 128], replicated, may hold values from -2 to 2
- point_matrix: bfloat16 [3, 128, 128], replicated, may hold values from -0.5 to 0.5
- ocean_gain: float32 [128], replicated, may hold values from 0.5 to 2
- ocean_qkv: bfloat16 [128, 384], replicated, may hold values from -0.5 to 0.5
- ocean_scale: float32 [2], replicated, may hold values from 4 to 32
- ocean_out: bfloat16 [128, 128], replicated, may hold values from -0.5 to 0.5
- seaside_return_matrix: bfloat16 [128, 384], replicated, may hold values from -0.5 to 0.5
Outputs:
- updated_airflow_field: bfloat16 [2, 16, 512, 384], P(None, 'lat', ('lon', 'comp'))
- updated_seaside_channels: bfloat16 [2, 16, 512, 128], P(None, 'lat', ('lon', 'comp'))
Inputs may be any that keep to these rules, and one draw needn't show every extreme that they name: `land_sea`: 1 marks a sea column, 0 land. `window_ids`: along each latitude the value is the longitude of the first column of that column's window; it never falls along a row, every window lies inside an aligned run of 128 longitudes, and the last longitude of every row is a window of its own.
All inputs are finite; a program needn't handle non-finite values. No bound on the sum of `land_sea` on one device may be relied on, other than what follows from the above.
Results may differ from a plain program's by a relative error of at most 0.018.
Values may be sent and summed in bfloat16 or wider, within the bound.
A program may use at most 64 MiB of HBM per device.

v0:
```python
import jax
import jax.numpy as jnp
from jax import lax
from jax.sharding import PartitionSpec as P

WIDTH = 384
HEADS = 6
OCEAN = 128
OHEADS = 2
BLOCKS = 2
COLS_DEV = 128


NORM_EPS = 1e-05
UNIT_EPS = 1e-06


def padded_2(block, sides, width, periodic):
    for axis, dim in sides:
        count = lax.axis_size(axis)
        forward = [(i, i + 1) for i in range(count - 1)]
        if periodic:
            forward.append((count - 1, 0))
        backward = [(target, source) for source, target in forward]
        low = lax.ppermute(
            lax.slice_in_dim(block, block.shape[dim] - width, None, axis=dim), axis, forward
        )
        high = lax.ppermute(lax.slice_in_dim(block, 0, width, axis=dim), axis, backward)
        block = jnp.concatenate([low, block, high], axis=dim)
    return block


def passed_along(value, axis, steps):
    count = lax.axis_size(axis)
    pairs = [(source, (source + steps) % count) for source in range(count)]
    return lax.ppermute(value, axis, pairs)


def damped_model_field(values_in):
    return lax.optimization_barrier(values_in.astype(jnp.bfloat16))


def smooth(values_in):
    return jax.nn.gelu(values_in, approximate=False)


def layer_norm(values_in, gain_vector):
    widened = values_in.astype(jnp.float32)
    centred = widened - jnp.mean(widened, axis=-1, keepdims=True)
    spread = jnp.mean(centred * centred, axis=-1, keepdims=True)
    return centred * lax.rsqrt(spread + NORM_EPS) * gain_vector


def unit_heads(projected, head_count):
    shaped = projected.reshape(
        projected.shape[:-1] + (head_count, projected.shape[-1] // head_count)
    )
    shaped = shaped * lax.rsqrt(jnp.mean(shaped * shaped, axis=-1, keepdims=True) + UNIT_EPS)
    return damped_model_field(shaped.reshape(projected.shape))


def nine_taps(padded, kernel):
    row_count = padded.shape[1] - 2
    col_count = padded.shape[2] - 2
    accum = jnp.zeros((padded.shape[0], row_count, col_count, padded.shape[3]), jnp.float32)
    for lat_shift in range(3):
        for lon_shift in range(3):
            window = padded[:, lat_shift : lat_shift + row_count, lon_shift : lon_shift + col_count]
            accum = accum + window.astype(jnp.float32) * kernel[lat_shift, lon_shift]
    return accum


def atm_conv(state_in, kernel):
    padded = padded_2(state_in, (("lat", 1),), 1, False)
    padded = padded_2(padded, ((("lon", "comp"), 2),), 1, True)
    return nine_taps(padded, kernel)


def piece_rims(values_in):
    lat_place = lax.axis_index("lat")
    lat_count = lax.axis_size("lat")
    near_left = passed_along(values_in[:, :, -1:], "lat", 1)
    far_left = passed_along(near_left, ("lon", "comp"), 1)
    left_col = jnp.where(lat_place == 0, far_left, near_left)
    near_right = passed_along(values_in[:, :, :1], "lat", -1)
    far_right = passed_along(near_right, ("lon", "comp"), -1)
    right_col = jnp.where(lat_place == lat_count - 1, far_right, near_right)
    return jnp.concatenate([left_col, values_in, right_col], axis=2)


def ocean_conv(values_in, kernel):
    padded = piece_rims(values_in)
    padded = jnp.pad(padded, ((0, 0), (1, 1), (0, 0), (0, 0)))
    return nine_taps(padded, kernel)


def window_attend(query_units, key_units, value_rows, window_ids, head_scale):
    members, row_count, length, channels = query_units.shape
    head_count = head_scale.shape[0]
    head_dim = channels // head_count
    blocks = length // COLS_DEV
    shape_six = (members, row_count, blocks, COLS_DEV, head_count, head_dim)
    query_six = query_units.reshape(shape_six)
    key_six = key_units.reshape(shape_six)
    value_six = value_rows.reshape(shape_six)
    id_blocks = window_ids.reshape(row_count, blocks, COLS_DEV)
    same_window = id_blocks[:, :, :, None] == id_blocks[:, :, None, :]
    scores = (
        jnp.einsum("mrbqhd,mrbkhd->mrbhqk", query_six, key_six, preferred_element_type=jnp.float32)
        * (head_scale / head_dim)[:, None, None]
    )
    exp_terms = jnp.where(same_window[None, :, :, None], jnp.exp(scores), 0.0)
    denominator = jnp.sum(exp_terms, axis=-1)
    numerator = jnp.einsum(
        "mrbhqk,mrbkhd->mrbqhd",
        damped_model_field(exp_terms),
        value_six,
        preferred_element_type=jnp.float32,
    )
    result = numerator / jnp.transpose(denominator, (0, 1, 2, 4, 3))[..., None]
    return damped_model_field(result.reshape(members, row_count, length, channels))


def token_section(
    mixed_state,
    window_ids,
    attn_gain,
    qkv_matrix,
    attn_scales,
    out_matrix,
    mlp_gain,
    scale_in,
    scale_out,
    up_matrix,
    down_matrix,
):
    normed = damped_model_field(layer_norm(mixed_state, attn_gain))
    projected = jnp.dot(normed, qkv_matrix, preferred_element_type=jnp.float32)
    query_units = unit_heads(projected[..., :WIDTH], HEADS)
    key_units = unit_heads(projected[..., WIDTH : 2 * WIDTH], HEADS)
    value_rows = damped_model_field(projected[..., 2 * WIDTH :])
    attended = window_attend(query_units, key_units, value_rows, window_ids, attn_scales)
    after_attn = damped_model_field(
        mixed_state.astype(jnp.float32)
        + jnp.dot(attended, out_matrix, preferred_element_type=jnp.float32)
    )
    scaled = damped_model_field(layer_norm(after_attn, mlp_gain) * scale_in[:, None, None, :])
    lifted_channel_values = (
        jnp.dot(scaled, up_matrix, preferred_element_type=jnp.float32) * scale_out[:, None, None, :]
    )
    activated = damped_model_field(smooth(lifted_channel_values))
    return damped_model_field(
        after_attn.astype(jnp.float32)
        + jnp.dot(activated, down_matrix, preferred_element_type=jnp.float32)
    )


def pool_pairs(values_in):
    members, row_count, col_count, channels = values_in.shape
    shaped = values_in.astype(jnp.float32).reshape(
        members, row_count // 2, 2, col_count // 2, 2, channels
    )
    return jnp.mean(shaped, axis=(2, 4))


def upsample(coarse):
    members, row_count, col_count, channels = coarse.shape
    spread_out = jnp.broadcast_to(
        coarse[:, :, None, :, None, :], (members, row_count, 2, col_count, 2, channels)
    )
    return spread_out.reshape(members, 2 * row_count, 2 * col_count, channels)


def lat_terms(query_units, key_units, value_rows, head_scale):
    head_count = head_scale.shape[0]
    head_dim = query_units.shape[-1] // head_count
    query_five = query_units.reshape(query_units.shape[:-1] + (head_count, head_dim))
    key_five = key_units.reshape(key_units.shape[:-1] + (head_count, head_dim))
    value_five = value_rows.reshape(key_units.shape[:-1] + (head_count, head_dim))
    scores = (
        jnp.einsum("mijhd,mkjhd->mhikj", query_five, key_five, preferred_element_type=jnp.float32)
        * (head_scale / head_dim)[None, :, None, None, None]
    )
    exp_terms = jnp.exp(scores)
    denominator = jnp.sum(exp_terms, axis=3)
    numerator = jnp.einsum(
        "mhikj,mkjhd->mijhd",
        damped_model_field(exp_terms),
        value_five,
        preferred_element_type=jnp.float32,
    )
    return (numerator, denominator)


def finish_heads(numerator, denominator):
    result = numerator / jnp.transpose(denominator, (0, 2, 3, 1))[..., None]
    return damped_model_field(
        result.reshape(result.shape[:3] + (result.shape[3] * result.shape[4],))
    )


def ocean_trunk(source, conv_ocean, point_matrix, ocean_gain, ocean_qkv, ocean_scale, ocean_out):
    act_first = damped_model_field(ocean_conv(source, conv_ocean[0]))
    fine_first = damped_model_field(
        smooth(jnp.dot(act_first, point_matrix[0], preferred_element_type=jnp.float32))
    )
    coarse_start = damped_model_field(pool_pairs(fine_first))
    act_second = damped_model_field(ocean_conv(coarse_start, conv_ocean[1]))
    coarse_first = damped_model_field(
        smooth(jnp.dot(act_second, point_matrix[1], preferred_element_type=jnp.float32))
    )
    normed = damped_model_field(layer_norm(coarse_first, ocean_gain))
    projected = jnp.dot(normed, ocean_qkv, preferred_element_type=jnp.float32)
    query_units = unit_heads(projected[..., :OCEAN], OHEADS)
    key_units = unit_heads(projected[..., OCEAN : 2 * OCEAN], OHEADS)
    value_rows = damped_model_field(projected[..., 2 * OCEAN :])
    numerator, denominator = lat_terms(query_units, key_units, value_rows, ocean_scale)
    attended = finish_heads(numerator, denominator)
    coarse_next = damped_model_field(
        coarse_first.astype(jnp.float32)
        + jnp.dot(attended, ocean_out, preferred_element_type=jnp.float32)
    )
    merged = damped_model_field(
        fine_first.astype(jnp.float32) + upsample(coarse_next).astype(jnp.float32)
    )
    return damped_model_field(ocean_conv(merged, conv_ocean[2]))


def per_device(
    atm_state,
    ocean_prev,
    land_sea,
    window_ids,
    conv_atm,
    attn_gain,
    qkv_matrix,
    attn_scales,
    out_matrix,
    mlp_gain,
    member_in,
    member_out,
    up_matrix,
    down_matrix,
    flux_matrix,
    conv_ocean,
    point_matrix,
    ocean_gain,
    ocean_qkv,
    ocean_scale,
    ocean_out,
    seaside_return_matrix,
):
    current_model_field = atm_state
    for block_index in range(BLOCKS):
        mixed_state = damped_model_field(
            current_model_field.astype(jnp.float32)
            + atm_conv(current_model_field, conv_atm[block_index])
        )
        current_model_field = token_section(
            mixed_state,
            window_ids,
            attn_gain[block_index],
            qkv_matrix[block_index],
            attn_scales[block_index],
            out_matrix[block_index],
            mlp_gain[block_index],
            member_in[block_index],
            member_out[block_index],
            up_matrix[block_index],
            down_matrix[block_index],
        )
    marine_grid_indicator = land_sea.astype(jnp.float32)[None, :, :, None]
    flux_terms = jnp.dot(current_model_field, flux_matrix, preferred_element_type=jnp.float32)
    marine_starting_field = damped_model_field(
        marine_grid_indicator * (ocean_prev.astype(jnp.float32) + flux_terms)
    )
    source = lax.all_to_all(marine_starting_field, "lat", split_axis=2, concat_axis=1, tiled=True)
    act_last = ocean_trunk(
        source, conv_ocean, point_matrix, ocean_gain, ocean_qkv, ocean_scale, ocean_out
    )
    act_last = lax.all_to_all(act_last, "lat", split_axis=1, concat_axis=2, tiled=True)
    lifted_channel_values = smooth(
        jnp.dot(act_last, point_matrix[2], preferred_element_type=jnp.float32)
    )
    updated_seaside_channels = damped_model_field(
        marine_grid_indicator * (marine_starting_field.astype(jnp.float32) + lifted_channel_values)
    )
    updated_airflow_field = damped_model_field(
        current_model_field.astype(jnp.float32)
        + marine_grid_indicator
        * jnp.dot(
            updated_seaside_channels, seaside_return_matrix, preferred_element_type=jnp.float32
        )
    )
    return (updated_airflow_field, updated_seaside_channels)


def solution(mesh):
    return jax.shard_map(
        per_device,
        mesh=mesh,
        in_specs=(
            P(None, "lat", ("lon", "comp"), None),
            P(None, "lat", ("lon", "comp"), None),
            P("lat", ("lon", "comp")),
            P("lat", ("lon", "comp")),
            P(),
            P(),
            P(),
            P(),
            P(),
            P(),
            P(),
            P(),
            P(),
            P(),
            P(),
            P(),
            P(),
            P(),
            P(),
            P(),
            P(),
            P(),
        ),
        out_specs=(P(None, "lat", ("lon", "comp"), None), P(None, "lat", ("lon", "comp"), None)),
        check_vma=False,
    )
```

profile of v0, /device:TPU:0, one launch (start us, length us, event | category | flops | bytes accessed | tf_op | source)
XLA Modules:
  0.0 168.9 jit_solution(2255840597637318369)
XLA Ops:
  0.7 1.1 fusion.163
  1.8 4.9 %collective-permute-start = (bf16[2,1,128,384]{3,2,1,0:T(8,128)(2,1)S(1)}, bf16[2,1,128,384]{3,2,1,0:T(8,128)(2,1)S(1)}, u32[]{:S(2)}, u32[]{:S(2)}) collective-permute-start(bf16[2,1,128,384]{3,2,1,0:T(8,128)(2,1)S(1)} %get-tuple-element.45), channel_id=1, source_target_pairs={{0,4},{4,8},{8,12},{12,16},{16,20},{20,24},{24,28},{1,5},{5,9},{9,... | collective-permute-start | bytes 589832 | tf_op jit(solution)/shard_map/ppermute | solution.py:25
  6.7 1.3 collective-permute-start.1
  8.0 0.8 fusion.168
  8.9 0.8 slice_reduce_fusion.19
  9.7 0.9 broadcast_compare_fusion
  12.0 0.8 multiply_bitcast_fusion
  12.8 1.2 constant_dynamic-update-slice_fusion.1
  14.0 1.0 collective-permute-done.1
  15.1 1.7 %collective-permute-start.3 = (bf16[2,4,1,384]{3,2,1,0:T(2,128)(2,1)S(1)}, bf16[2,4,1,384]{3,2,1,0:T(2,128)(2,1)S(1)}, u32[]{:S(2)}, u32[]{:S(2)}) collective-permute-start(bf16[2,4,1,384]{3,2,1,0:T(2,128)(2,1)S(1)} %get-tuple-element.41), channel_id=1, source_target_pairs={{1,0},{2,1},{3,2},{0,3},{5,4},{6,5},{7,6},{4,7},{9,8},{10,9},{11,1... | collective-permute-start | bytes 18440 | tf_op jit(solution)/shard_map/ppermute | solution.py:28
  16.8 1.4 collective-permute-done.2
  18.2 0.9 fusion.78
  19.8 0.8 fusion.55
  20.6 1.3 slice_multiply_fusion.2
  21.9 2.3 %copy.66 = f32[2,2,128,384]{2,3,1,0:T(8,128)} copy(f32[2,2,128,384]{3,2,1,0:T(8,128)} %get-tuple-element.31) | data formatting | bytes 1572864 | tf_op jit(solution)/shard_map/mul | solution.py:58
  24.2 1.2 reduce_sum.186
  25.4 0.9 mul.842
  26.3 2.3 %copy.67 = f32[2,2,128,384]{3,2,1,0:T(8,128)} copy(f32[2,2,128,384]{2,3,1,0:T(8,128)} %bitcast.277) | data formatting | bytes 1572864 | tf_op jit(solution)/shard_map/mul | solution.py:58
  28.6 2.3 %copy.69 = f32[2,2,128,384]{2,3,1,0:T(8,128)} copy(f32[2,2,128,384]{3,2,1,0:T(8,128)} %get-tuple-element.30) | data formatting | bytes 1572864 | tf_op jit(solution)/shard_map/mul | solution.py:58
  30.9 1.2 reduce_sum.187
  32.1 0.9 mul.847
  33.1 2.3 %copy.70 = f32[2,2,128,384]{3,2,1,0:T(8,128)} copy(f32[2,2,128,384]{2,3,1,0:T(8,128)} %bitcast.279) | data formatting | bytes 1572864 | tf_op jit(solution)/shard_map/mul | solution.py:58
  35.4 2.4 %multiply_convert_fusion.2 = (bf16[2,2,128,384]{3,2,1,0:T(8,128)(2,1)}, bf16[2,2,128,384]{3,2,1,0:T(8,128)(2,1)}) fusion(f32[2,2,128,384]{3,2,1,0:T(8,128)} %copy.70, f32[2,2,128,1152]{3,2,1,0:T(8,128)S(1)} %fusion.55, f32[2,2,128,384]{3,2,1,0:T(8,128)} %copy.67), kind=kLoop, calls=%fused_computation.144 | loop fusion | flops 786432 | bytes 3932160 | tf_op jit(solution)/shard_map/convert_element_type | solution.py:40
  37.8 1.2 copy.68
  39.0 1.2 copy.71
  43.1 8.0 %fusion.2 = bf16[2,2,128,1536]{3,2,1,0:T(8,128)(2,1)S(1)} fusion(bf16[2,2,128,384]{3,2,1,0:T(8,128)(2,1)S(1)} %fusion.69, f32[2,1536]{1,0:T(2,128)S(1)} %get-tuple-element.61, bf16[2,384,1536]{2,1,0:T(8,128)(2,1)S(1)} %copy-done.15), kind=kOutput, calls=%fused_computation.6 | convolution fusion | flops 655884288 | bytes 3158016 | tf_op jit(solution)/shard_map/dot_general | solution.py:149
  51.2 1.0 fusion.23
  52.3 5.7 %collective-permute-start.4 = (bf16[2,1,128,384]{3,2,1,0:T(8,128)(2,1)S(1)}, bf16[2,1,128,384]{3,2,1,0:T(8,128)(2,1)S(1)}, u32[]{:S(2)}, u32[]{:S(2)}) collective-permute-start(bf16[2,1,128,384]{3,2,1,0:T(8,128)(2,1)S(1)} %get-tuple-element.42), channel_id=1, source_target_pairs={{0,4},{4,8},{8,12},{12,16},{16,20},{20,24},{24,28},{1,5},{5,9},{9,... | collective-permute-start | bytes 589832 | tf_op jit(solution)/shard_map/ppermute | solution.py:25
  58.0 1.3 collective-permute-start.5
  59.3 3.4 %collective-permute-done.4 = bf16[2,1,128,384]{3,2,1,0:T(8,128)(2,1)S(1)} collective-permute-done((bf16[2,1,128,384]{3,2,1,0:T(8,128)(2,1)S(1)}, bf16[2,1,128,384]{3,2,1,0:T(8,128)(2,1)S(1)}, u32[]{:S(2)}, u32[]{:S(2)}) %collective-permute-start.4) | collective-permute-done | bytes 196640 | tf_op jit(solution)/shard_map/ppermute | solution.py:25
  62.7 4.6 %collective-permute-done.5 = bf16[2,1,128,384]{3,2,1,0:T(8,128)(2,1)S(1)} collective-permute-done((bf16[2,1,128,384]{3,2,1,0:T(8,128)(2,1)S(1)}, bf16[2,1,128,384]{3,2,1,0:T(8,128)(2,1)S(1)}, u32[]{:S(2)}, u32[]{:S(2)}) %collective-permute-start.5) | collective-permute-done | bytes 196640 | tf_op jit(solution)/shard_map/ppermute | solution.py:28
  67.6 1.6 collective-permute-start.7
  69.2 1.3 collective-permute-done.6
  70.9 0.8 fusion.84
  72.4 0.8 fusion.53
  73.2 1.3 slice_multiply_fusion
  74.5 2.3 %copy.75 = f32[2,2,128,384]{2,3,1,0:T(8,128)} copy(f32[2,2,128,384]{3,2,1,0:T(8,128)} %get-tuple-element.27) | data formatting | bytes 1572864 | tf_op jit(solution)/shard_map/mul | solution.py:58
  76.8 1.2 reduce_sum.194
  78.0 0.9 mul.902
  79.0 2.3 %copy.76 = f32[2,2,128,384]{3,2,1,0:T(8,128)} copy(f32[2,2,128,384]{2,3,1,0:T(8,128)} %bitcast.281) | data formatting | bytes 1572864 | tf_op jit(solution)/shard_map/mul | solution.py:58
  81.2 2.3 %copy.78 = f32[2,2,128,384]{2,3,1,0:T(8,128)} copy(f32[2,2,128,384]{3,2,1,0:T(8,128)} %get-tuple-element.26) | data formatting | bytes 1572864 | tf_op jit(solution)/shard_map/mul | solution.py:58
  83.5 1.2 reduce_sum.195
  84.8 0.9 mul.907
  85.7 2.3 %copy.79 = f32[2,2,128,384]{3,2,1,0:T(8,128)} copy(f32[2,2,128,384]{2,3,1,0:T(8,128)} %bitcast.283) | data formatting | bytes 1572864 | tf_op jit(solution)/shard_map/mul | solution.py:58
  88.0 2.4 %multiply_convert_fusion = (bf16[2,2,128,384]{3,2,1,0:T(8,128)(2,1)}, bf16[2,2,128,384]{3,2,1,0:T(8,128)(2,1)}) fusion(f32[2,2,128,384]{3,2,1,0:T(8,128)} %copy.79, f32[2,2,128,1152]{3,2,1,0:T(8,128)S(1)} %fusion.53, f32[2,2,128,384]{3,2,1,0:T(8,128)} %copy.76), kind=kLoop, calls=%fused_computation.141 | loop fusion | flops 786432 | bytes 3932160 | tf_op jit(solution)/shard_map/convert_element_type | solution.py:40
  90.4 1.2 copy.77
  91.6 1.2 copy.80
  95.8 8.0 %fusion.5 = bf16[2,2,128,1536]{3,2,1,0:T(8,128)(2,1)S(1)} fusion(bf16[2,2,128,384]{3,2,1,0:T(8,128)(2,1)S(1)} %fusion.62, f32[2,1536]{1,0:T(2,128)S(1)} %get-tuple-element.60, bf16[2,384,1536]{2,1,0:T(8,128)(2,1)S(1)} %copy-done.16), kind=kOutput, calls=%fused_computation.9 | convolution fusion | flops 655884288 | bytes 3158016 | tf_op jit(solution)/shard_map/dot_general | solution.py:149
  103.9 1.0 fusion.25
  105.3 14.5 %all_to_all.36 = bf16[2,2,128,128]{3,1,0,2:T(2,128)(2,1)S(1)} all-to-all(bf16[2,2,128,128]{3,1,0,2:T(2,128)(2,1)S(1)} %copy.83), channel_id=1, replica_groups=mesh['lat'=8,'lon'=2,'comp'=2] {'lat'}, dimensions={2} | all-to-all | bytes 262144 | tf_op jit(solution)/shard_map/all_to_all | solution.py:277
  119.9 4.7 %collective-permute-start.10 = (bf16[2,16,1,128]{3,2,1,0:T(2,128)(2,1)S(1)}, bf16[2,16,1,128]{3,2,1,0:T(2,128)(2,1)S(1)}, u32[]{:S(2)}, u32[]{:S(2)}) collective-permute-start(bf16[2,16,1,128]{3,2,1,0:T(2,128)(2,1)S(1)} %get-tuple-element.55), channel_id=1, source_target_pairs={{0,28},{4,0},{8,4},{12,8},{16,12},{20,16},{24,20},{28,24},{1,29},{... | collective-permute-start | bytes 24584 | tf_op jit(solution)/shard_map/ppermute | solution.py:36
  124.6 1.7 %collective-permute-done.8 = bf16[2,16,1,128]{3,2,1,0:T(2,128)(2,1)S(1)} collective-permute-done((bf16[2,16,1,128]{3,2,1,0:T(2,128)(2,1)S(1)}, bf16[2,16,1,128]{3,2,1,0:T(2,128)(2,1)S(1)}, u32[]{:S(2)}, u32[]{:S(2)}) %collective-permute-start.8) | collective-permute-done | bytes 8224 | tf_op jit(solution)/shard_map/ppermute | solution.py:36
  126.4 1.8 %collective-permute-start.11 = (bf16[2,16,1,128]{3,2,1,0:T(2,128)(2,1)S(1)}, bf16[2,16,1,128]{3,2,1,0:T(2,128)(2,1)S(1)}, u32[]{:S(2)}, u32[]{:S(2)}) collective-permute-start(bf16[2,16,1,128]{3,2,1,0:T(2,128)(2,1)S(1)} %collective-permute-done.10), channel_id=1, source_target_pairs={{0,3},{1,0},{2,1},{3,2},{4,7},{5,4},{6,5},{7,6},{8,11},{9,8},{10,9... | collective-permute-start | bytes 24584 | tf_op jit(solution)/shard_map/ppermute | solution.py:36
  128.2 1.4 collective-permute-done.9
  131.2 4.7 %collective-permute-start.14 = (bf16[2,8,1,128]{3,2,1,0:T(2,128)(2,1)S(1)}, bf16[2,8,1,128]{3,2,1,0:T(2,128)(2,1)S(1)}, u32[]{:S(2)}, u32[]{:S(2)}) collective-permute-start(bf16[2,8,1,128]{3,2,1,0:T(2,128)(2,1)S(1)} %get-tuple-element.57), channel_id=1, source_target_pairs={{0,28},{4,0},{8,4},{12,8},{16,12},{20,16},{24,20},{28,24},{1,29},{... | collective-permute-start | bytes 12296 | tf_op jit(solution)/shard_map/ppermute | solution.py:36
  135.9 1.6 collective-permute-done.12
  137.6 1.9 %collective-permute-start.15 = (bf16[2,8,1,128]{3,2,1,0:T(2,128)(2,1)S(1)}, bf16[2,8,1,128]{3,2,1,0:T(2,128)(2,1)S(1)}, u32[]{:S(2)}, u32[]{:S(2)}) collective-permute-start(bf16[2,8,1,128]{3,2,1,0:T(2,128)(2,1)S(1)} %collective-permute-done.14), channel_id=1, source_target_pairs={{0,3},{1,0},{2,1},{3,2},{4,7},{5,4},{6,5},{7,6},{8,11},{9,8},{10,9... | collective-permute-start | bytes 12296 | tf_op jit(solution)/shard_map/ppermute | solution.py:36
  139.5 1.0 collective-permute-done.13
  144.7 4.7 %collective-permute-start.18 = (bf16[2,16,1,128]{3,2,1,0:T(2,128)(2,1)S(1)}, bf16[2,16,1,128]{3,2,1,0:T(2,128)(2,1)S(1)}, u32[]{:S(2)}, u32[]{:S(2)}) collective-permute-start(bf16[2,16,1,128]{3,2,1,0:T(2,128)(2,1)S(1)} %get-tuple-element.51), channel_id=1, source_target_pairs={{0,28},{4,0},{8,4},{12,8},{16,12},{20,16},{24,20},{28,24},{1,29},{... | collective-permute-start | bytes 24584 | tf_op jit(solution)/shard_map/ppermute | solution.py:36
  149.4 1.7 %collective-permute-done.16 = bf16[2,16,1,128]{3,2,1,0:T(2,128)(2,1)S(1)} collective-permute-done((bf16[2,16,1,128]{3,2,1,0:T(2,128)(2,1)S(1)}, bf16[2,16,1,128]{3,2,1,0:T(2,128)(2,1)S(1)}, u32[]{:S(2)}, u32[]{:S(2)}) %collective-permute-start.16) | collective-permute-done | bytes 8224 | tf_op jit(solution)/shard_map/ppermute | solution.py:36
  151.2 1.7 collective-permute-start.19
  152.9 1.4 collective-permute-done.17
  154.9 12.2 %all_to_all.37 = bf16[2,16,16,128]{3,2,0,1:T(8,128)(2,1)S(1)} all-to-all(bf16[2,16,16,128]{3,2,0,1:T(8,128)(2,1)S(1)} %copy.91), channel_id=1, replica_groups=mesh['lat'=8,'lon'=2,'comp'=2] {'lat'}, dimensions={1} | all-to-all | bytes 262144 | tf_op jit(solution)/shard_map/all_to_all | solution.py:281
  167.9 1.0 fusion.21
  (166 shorter events, 17.2 us)
Async XLA Ops:
  0.6 167.2 %copy-start = (bf16[128,384]{1,0:T(8,128)(2,1)S(1)}, bf16[128,384]{1,0:T(8,128)(2,1)}, u32[]{:S(2)}) copy-start(bf16[128,384]{1,0:T(8,128)(2,1)} %param.43) | copy-start | bytes 294916
  0.6 17.6 %copy-start.1 = (bf16[2,2,128,384]{3,2,1,0:T(8,128)(2,1)S(1)}, bf16[2,2,128,384]{3,2,1,0:T(8,128)(2,1)}, u32[]{:S(2)}) copy-start(bf16[2,2,128,384]{3,2,1,0:T(8,128)(2,1)} %param.22) | copy-start | bytes 1179652
  0.7 16.1 %copy-start.12 = (f32[2,384]{1,0:T(2,128)S(1)}, f32[2,384]{1,0:T(2,128)}, u32[]{:S(2)}) copy-start(f32[2,384]{1,0:T(2,128)} %param.31) | copy-start | bytes 9220
  1.8 10.9 %collective-permute-start = (bf16[2,1,128,384]{3,2,1,0:T(8,128)(2,1)S(1)}, bf16[2,1,128,384]{3,2,1,0:T(8,128)(2,1)S(1)}, u32[]{:S(2)}, u32[]{:S(2)}) collective-permute-start(bf16[2,1,128,384]{3,2,1,0:T(8,128)(2,1)S(1)} %get-tuple-element.45), channel_id=1, source_target_pairs={{0,4},{4,8},{8,12},{12,16},{16,20},{20,24},{24,28},{1,5},{5,9},{9,... | collective-permute-start | bytes 589832 | tf_op jit(solution)/shard_map/ppermute | solution.py:25
  6.7 8.3 %collective-permute-start.1 = (bf16[2,1,128,384]{3,2,1,0:T(8,128)(2,1)S(1)}, bf16[2,1,128,384]{3,2,1,0:T(8,128)(2,1)S(1)}, u32[]{:S(2)}, u32[]{:S(2)}) collective-permute-start(bf16[2,1,128,384]{3,2,1,0:T(8,128)(2,1)S(1)} %get-tuple-element.44), channel_id=1, source_target_pairs={{4,0},{8,4},{12,8},{16,12},{20,16},{24,20},{28,24},{5,1},{9,5},{13... | collective-permute-start | bytes 589832 | tf_op jit(solution)/shard_map/ppermute | solution.py:28
  12.8 7.0 %copy-start.2 = (bf16[2,384,1152]{2,1,0:T(8,128)(2,1)S(1)}, bf16[2,384,1152]{2,1,0:T(8,128)(2,1)}, u32[]{:S(2)}) copy-start(bf16[2,384,1152]{2,1,0:T(8,128)(2,1)} %param.28) | copy-start | bytes 5308420
  15.0 3.2 %collective-permute-start.2 = (bf16[2,4,1,384]{3,2,1,0:T(2,128)(2,1)S(1)}, bf16[2,4,1,384]{3,2,1,0:T(2,128)(2,1)S(1)}, u32[]{:S(2)}, u32[]{:S(2)}) collective-permute-start(bf16[2,4,1,384]{3,2,1,0:T(2,128)(2,1)S(1)} %get-tuple-element.40), channel_id=1, source_target_pairs={{0,1},{1,2},{2,3},{3,0},{4,5},{5,6},{6,7},{7,4},{8,9},{9,10},{10,1... | collective-permute-start | bytes 18440 | tf_op jit(solution)/shard_map/ppermute | solution.py:25
  15.1 3.1 %collective-permute-start.3 = (bf16[2,4,1,384]{3,2,1,0:T(2,128)(2,1)S(1)}, bf16[2,4,1,384]{3,2,1,0:T(2,128)(2,1)S(1)}, u32[]{:S(2)}, u32[]{:S(2)}) collective-permute-start(bf16[2,4,1,384]{3,2,1,0:T(2,128)(2,1)S(1)} %get-tuple-element.41), channel_id=1, source_target_pairs={{1,0},{2,1},{3,2},{0,3},{5,4},{6,5},{7,6},{4,7},{9,8},{10,9},{11,1... | collective-permute-start | bytes 18440 | tf_op jit(solution)/shard_map/ppermute | solution.py:28
  40.8 1.1 copy-start.4
  41.4 1.7 %copy-start.15 = (bf16[2,384,1536]{2,1,0:T(8,128)(2,1)S(1)}, bf16[2,384,1536]{2,1,0:T(8,128)(2,1)}, u32[]{:S(2)}) copy-start(bf16[2,384,1536]{2,1,0:T(8,128)(2,1)} %param.34) | copy-start | bytes 7077892
  43.1 8.1 %copy-start.17 = (bf16[2,1536,384]{2,1,0:T(8,128)(2,1)S(1)}, bf16[2,1536,384]{2,1,0:T(8,128)(2,1)}, u32[]{:S(2)}) copy-start(bf16[2,1536,384]{2,1,0:T(8,128)(2,1)} %param.35) | copy-start | bytes 7077892
  51.2 18.0 %copy-start.13 = (s32[2,128]{1,0:T(2,128)S(1)}, s32[2,128]{1,0:T(2,128)}, u32[]{:S(2)}) copy-start(s32[2,128]{1,0:T(2,128)} %param.24) | copy-start | bytes 3076
  52.3 10.4 %collective-permute-start.4 = (bf16[2,1,128,384]{3,2,1,0:T(8,128)(2,1)S(1)}, bf16[2,1,128,384]{3,2,1,0:T(8,128)(2,1)S(1)}, u32[]{:S(2)}, u32[]{:S(2)}) collective-permute-start(bf16[2,1,128,384]{3,2,1,0:T(8,128)(2,1)S(1)} %get-tuple-element.42), channel_id=1, source_target_pairs={{0,4},{4,8},{8,12},{12,16},{16,20},{20,24},{24,28},{1,5},{5,9},{9,... | collective-permute-start | bytes 589832 | tf_op jit(solution)/shard_map/ppermute | solution.py:25
  58.0 9.3 %collective-permute-start.5 = (bf16[2,1,128,384]{3,2,1,0:T(8,128)(2,1)S(1)}, bf16[2,1,128,384]{3,2,1,0:T(8,128)(2,1)S(1)}, u32[]{:S(2)}, u32[]{:S(2)}) collective-permute-start(bf16[2,1,128,384]{3,2,1,0:T(8,128)(2,1)S(1)} %get-tuple-element.43), channel_id=1, source_target_pairs={{4,0},{8,4},{12,8},{16,12},{20,16},{24,20},{28,24},{5,1},{9,5},{13... | collective-permute-start | bytes 589832 | tf_op jit(solution)/shard_map/ppermute | solution.py:28
  67.4 3.2 %collective-permute-start.6 = (bf16[2,4,1,384]{3,2,1,0:T(2,128)(2,1)S(1)}, bf16[2,4,1,384]{3,2,1,0:T(2,128)(2,1)S(1)}, u32[]{:S(2)}, u32[]{:S(2)}) collective-permute-start(bf16[2,4,1,384]{3,2,1,0:T(2,128)(2,1)S(1)} %get-tuple-element.38), channel_id=1, source_target_pairs={{0,1},{1,2},{2,3},{3,0},{4,5},{5,6},{6,7},{7,4},{8,9},{9,10},{10,1... | collective-permute-start | bytes 18440 | tf_op jit(solution)/shard_map/ppermute | solution.py:25
  67.6 3.0 %collective-permute-start.7 = (bf16[2,4,1,384]{3,2,1,0:T(2,128)(2,1)S(1)}, bf16[2,4,1,384]{3,2,1,0:T(2,128)(2,1)S(1)}, u32[]{:S(2)}, u32[]{:S(2)}) collective-permute-start(bf16[2,4,1,384]{3,2,1,0:T(2,128)(2,1)S(1)} %get-tuple-element.39), channel_id=1, source_target_pairs={{1,0},{2,1},{3,2},{0,3},{5,4},{6,5},{7,6},{4,7},{9,8},{10,9},{11,1... | collective-permute-start | bytes 18440 | tf_op jit(solution)/shard_map/ppermute | solution.py:28
  70.9 1.5 copy-start.3
  93.5 1.1 copy-start.5
  94.1 1.7 %copy-start.16 = (bf16[2,384,1536]{2,1,0:T(8,128)(2,1)S(1)}, bf16[2,384,1536]{2,1,0:T(8,128)(2,1)}, u32[]{:S(2)}) copy-start(bf16[2,384,1536]{2,1,0:T(8,128)(2,1)} %param.34) | copy-start | bytes 7077892
  95.8 8.1 %copy-start.18 = (bf16[2,1536,384]{2,1,0:T(8,128)(2,1)S(1)}, bf16[2,1536,384]{2,1,0:T(8,128)(2,1)}, u32[]{:S(2)}) copy-start(bf16[2,1536,384]{2,1,0:T(8,128)(2,1)} %param.35) | copy-start | bytes 7077892
  103.8 1.0 copy-start.7
  103.8 1.0 copy-start.9
  103.9 16.1 %copy-start.11 = (f32[3,3,3,128]{3,2,1,0:T(4,128)S(1)}, f32[3,3,3,128]{3,2,1,0:T(4,128)}, u32[]{:S(2)}) copy-start(f32[3,3,3,128]{3,2,1,0:T(4,128)} %param.37) | copy-start | bytes 41476
  104.9 25.2 %copy-start.19 = (bf16[3,128,128]{2,1,0:T(8,128)(2,1)S(1)}, bf16[3,128,128]{2,1,0:T(8,128)(2,1)}, u32[]{:S(2)}) copy-start(bf16[3,128,128]{2,1,0:T(8,128)(2,1)} %param.38) | copy-start | bytes 294916
  119.9 6.5 %collective-permute-start.8 = (bf16[2,16,1,128]{3,2,1,0:T(2,128)(2,1)S(1)}, bf16[2,16,1,128]{3,2,1,0:T(2,128)(2,1)S(1)}, u32[]{:S(2)}, u32[]{:S(2)}) collective-permute-start(bf16[2,16,1,128]{3,2,1,0:T(2,128)(2,1)S(1)} %get-tuple-element.54), channel_id=1, source_target_pairs={{0,4},{4,8},{8,12},{12,16},{16,20},{20,24},{24,28},{28,0},{1,5},{5... | collective-permute-start | bytes 24584 | tf_op jit(solution)/shard_map/ppermute | solution.py:36
  119.9 6.4 %collective-permute-start.10 = (bf16[2,16,1,128]{3,2,1,0:T(2,128)(2,1)S(1)}, bf16[2,16,1,128]{3,2,1,0:T(2,128)(2,1)S(1)}, u32[]{:S(2)}, u32[]{:S(2)}) collective-permute-start(bf16[2,16,1,128]{3,2,1,0:T(2,128)(2,1)S(1)} %get-tuple-element.55), channel_id=1, source_target_pairs={{0,28},{4,0},{8,4},{12,8},{16,12},{20,16},{24,20},{28,24},{1,29},{... | collective-permute-start | bytes 24584 | tf_op jit(solution)/shard_map/ppermute | solution.py:36
  126.3 3.2 %collective-permute-start.9 = (bf16[2,16,1,128]{3,2,1,0:T(2,128)(2,1)S(1)}, bf16[2,16,1,128]{3,2,1,0:T(2,128)(2,1)S(1)}, u32[]{:S(2)}, u32[]{:S(2)}) collective-permute-start(bf16[2,16,1,128]{3,2,1,0:T(2,128)(2,1)S(1)} %collective-permute-done.8), channel_id=1, source_target_pairs={{0,1},{1,2},{2,3},{3,0},{4,5},{5,6},{6,7},{7,4},{8,9},{9,10},{10,1... | collective-permute-start | bytes 24584 | tf_op jit(solution)/shard_map/ppermute | solution.py:36
  126.4 3.2 %collective-permute-start.11 = (bf16[2,16,1,128]{3,2,1,0:T(2,128)(2,1)S(1)}, bf16[2,16,1,128]{3,2,1,0:T(2,128)(2,1)S(1)}, u32[]{:S(2)}, u32[]{:S(2)}) collective-permute-start(bf16[2,16,1,128]{3,2,1,0:T(2,128)(2,1)S(1)} %collective-permute-done.10), channel_id=1, source_target_pairs={{0,3},{1,0},{2,1},{3,2},{4,7},{5,4},{6,5},{7,6},{8,11},{9,8},{10,9... | collective-permute-start | bytes 24584 | tf_op jit(solution)/shard_map/ppermute | solution.py:36
  130.1 7.5 %copy-start.20 = (f32[2]{0:T(128)S(1)}, f32[2]{0:T(128)}, u32[]{:S(2)}) copy-start(f32[2]{0:T(128)} %param.41) | copy-start | bytes 28
  130.8 10.8 %copy-start.14 = (f32[128]{0:T(128)S(1)}, f32[128]{0:T(128)}, u32[]{:S(2)}) copy-start(f32[128]{0:T(128)} %param.39) | copy-start | bytes 1540
  130.8 10.9 %copy-start.8 = (bf16[128,384]{1,0:T(8,128)(2,1)S(1)}, bf16[128,384]{1,0:T(8,128)(2,1)}, u32[]{:S(2)}) copy-start(bf16[128,384]{1,0:T(8,128)(2,1)} %param.40) | copy-start | bytes 294916
  131.1 6.4 %collective-permute-start.12 = (bf16[2,8,1,128]{3,2,1,0:T(2,128)(2,1)S(1)}, bf16[2,8,1,128]{3,2,1,0:T(2,128)(2,1)S(1)}, u32[]{:S(2)}, u32[]{:S(2)}) collective-permute-start(bf16[2,8,1,128]{3,2,1,0:T(2,128)(2,1)S(1)} %get-tuple-element.56), channel_id=1, source_target_pairs={{0,4},{4,8},{8,12},{12,16},{16,20},{20,24},{24,28},{28,0},{1,5},{5... | collective-permute-start | bytes 12296 | tf_op jit(solution)/shard_map/ppermute | solution.py:36
  131.2 6.4 %collective-permute-start.14 = (bf16[2,8,1,128]{3,2,1,0:T(2,128)(2,1)S(1)}, bf16[2,8,1,128]{3,2,1,0:T(2,128)(2,1)S(1)}, u32[]{:S(2)}, u32[]{:S(2)}) collective-permute-start(bf16[2,8,1,128]{3,2,1,0:T(2,128)(2,1)S(1)} %get-tuple-element.57), channel_id=1, source_target_pairs={{0,28},{4,0},{8,4},{12,8},{16,12},{20,16},{24,20},{28,24},{1,29},{... | collective-permute-start | bytes 12296 | tf_op jit(solution)/shard_map/ppermute | solution.py:36
  137.5 3.1 %collective-permute-start.13 = (bf16[2,8,1,128]{3,2,1,0:T(2,128)(2,1)S(1)}, bf16[2,8,1,128]{3,2,1,0:T(2,128)(2,1)S(1)}, u32[]{:S(2)}, u32[]{:S(2)}) collective-permute-start(bf16[2,8,1,128]{3,2,1,0:T(2,128)(2,1)S(1)} %collective-permute-done.12), channel_id=1, source_target_pairs={{0,1},{1,2},{2,3},{3,0},{4,5},{5,6},{6,7},{7,4},{8,9},{9,10},{10,1... | collective-permute-start | bytes 12296 | tf_op jit(solution)/shard_map/ppermute | solution.py:36
  137.6 3.3 %collective-permute-start.15 = (bf16[2,8,1,128]{3,2,1,0:T(2,128)(2,1)S(1)}, bf16[2,8,1,128]{3,2,1,0:T(2,128)(2,1)S(1)}, u32[]{:S(2)}, u32[]{:S(2)}) collective-permute-start(bf16[2,8,1,128]{3,2,1,0:T(2,128)(2,1)S(1)} %collective-permute-done.14), channel_id=1, source_target_pairs={{0,3},{1,0},{2,1},{3,2},{4,7},{5,4},{6,5},{7,6},{8,11},{9,8},{10,9... | collective-permute-start | bytes 12296 | tf_op jit(solution)/shard_map/ppermute | solution.py:36
  141.8 2.5 %copy-start.10 = (bf16[128,128]{1,0:T(8,128)(2,1)S(1)}, bf16[128,128]{1,0:T(8,128)(2,1)}, u32[]{:S(2)}) copy-start(bf16[128,128]{1,0:T(8,128)(2,1)} %param.42) | copy-start | bytes 98308
  144.6 6.5 %collective-permute-start.16 = (bf16[2,16,1,128]{3,2,1,0:T(2,128)(2,1)S(1)}, bf16[2,16,1,128]{3,2,1,0:T(2,128)(2,1)S(1)}, u32[]{:S(2)}, u32[]{:S(2)}) collective-permute-start(bf16[2,16,1,128]{3,2,1,0:T(2,128)(2,1)S(1)} %get-tuple-element.50), channel_id=1, source_target_pairs={{0,4},{4,8},{8,12},{12,16},{16,20},{20,24},{24,28},{28,0},{1,5},{5... | collective-permute-start | bytes 24584 | tf_op jit(solution)/shard_map/ppermute | solution.py:36
  144.7 6.6 %collective-permute-start.18 = (bf16[2,16,1,128]{3,2,1,0:T(2,128)(2,1)S(1)}, bf16[2,16,1,128]{3,2,1,0:T(2,128)(2,1)S(1)}, u32[]{:S(2)}, u32[]{:S(2)}) collective-permute-start(bf16[2,16,1,128]{3,2,1,0:T(2,128)(2,1)S(1)} %get-tuple-element.51), channel_id=1, source_target_pairs={{0,28},{4,0},{8,4},{12,8},{16,12},{20,16},{24,20},{28,24},{1,29},{... | collective-permute-start | bytes 24584 | tf_op jit(solution)/shard_map/ppermute | solution.py:36
  151.1 3.2 %collective-permute-start.17 = (bf16[2,16,1,128]{3,2,1,0:T(2,128)(2,1)S(1)}, bf16[2,16,1,128]{3,2,1,0:T(2,128)(2,1)S(1)}, u32[]{:S(2)}, u32[]{:S(2)}) collective-permute-start(bf16[2,16,1,128]{3,2,1,0:T(2,128)(2,1)S(1)} %collective-permute-done.16), channel_id=1, source_target_pairs={{0,1},{1,2},{2,3},{3,0},{4,5},{5,6},{6,7},{7,4},{8,9},{9,10},{10,1... | collective-permute-start | bytes 24584 | tf_op jit(solution)/shard_map/ppermute | solution.py:36
  151.2 3.1 %collective-permute-start.19 = (bf16[2,16,1,128]{3,2,1,0:T(2,128)(2,1)S(1)}, bf16[2,16,1,128]{3,2,1,0:T(2,128)(2,1)S(1)}, u32[]{:S(2)}, u32[]{:S(2)}) collective-permute-start(bf16[2,16,1,128]{3,2,1,0:T(2,128)(2,1)S(1)} %collective-permute-done.18), channel_id=1, source_target_pairs={{0,3},{1,0},{2,1},{3,2},{4,7},{5,4},{6,5},{7,6},{8,11},{9,8},{10,9... | collective-permute-start | bytes 24584 | tf_op jit(solution)/shard_map/ppermute | solution.py:36
  167.9 1.0 copy-start.6
where the time goes:
time: 170 us; the launch traced here: 169 us
  starting transfers between devices  36.7 us (22%)
  local copies, waits for them, and re-layouts  36 us (21%)
  blocking collectives  26.7 us (16%)
  matrix products  26.2 us (15%)
  waiting for transfers between devices  20.9 us (12%)
  other arithmetic  20.7 us (12%)
    ppermute x12, starting transfers between devices, passed_along(): return lax.ppermute(value, axis, pairs)  19.9 us
    dot_general x2, matrix products, token_section(): jnp.dot(scaled, up_matrix, preferred_element_type=jnp.float32)  16.1 us
    all_to_all x1, blocking collectives, per_device(): lax.all_to_all(marine_starting_field, 'lat', split_axis=2, concat_axis=1,...  14.5 us
    mul x12, local copies, waits for them, and re-layouts, unit_heads(): shaped * lax.rsqrt(jnp.mean(shaped * shaped, axis=-1, keepdims=True) + UN...  13.6 us
    all_to_all x1, blocking collectives, per_device(): lax.all_to_all(act_last, 'lat', split_axis=1, concat_axis=2, tiled=True)  12.2 us
    ppermute x4, starting transfers between devices, padded_2(): lax.ppermute(lax.slice_in_dim(block, block.shape[dim] - width, None, axis...  10.9 us
    mul x6, local copies, waits for them, and re-layouts, unit_heads(): shaped * shaped  9.42 us
    ppermute x12, waiting for transfers between devices, passed_along(): return lax.ppermute(value, axis, pairs)  9.22 us
  transfers between devices with their start and end apart: 20, of which 14 were waited for; matrix products, arithmetic and copies ran while one was open for 4% of the time, Pallas kernels for 0%

commit v1 on v0

v1 whole, which is shorter than its diff:
```python
import functools

import jax
import jax.numpy as jnp
from jax import lax
from jax.experimental import pallas as pl
from jax.experimental.pallas import tpu as pltpu
from jax.sharding import PartitionSpec as P

NORM_EPS = 1e-05
UNIT_EPS = 1e-06
HEAD = 64
LANES = 128
RIM = 8
EDGE = 16
LOG2E = 1.4426950408889634
MESH = pl.DeviceIdType.MESH
F32 = jnp.float32
BF16 = jnp.bfloat16
SIDES = [(dy, dx) for dy in (-1, 0, 1) for dx in (-1, 0, 1) if (dy, dx) != (0, 0)]


def gelu(x):
    return 0.5 * x * (1.0 + lax.erf(x * 0.7071067811865476))


def layer_norm(x, gain):
    centred = x - jnp.mean(x, axis=-1, keepdims=True)
    spread = jnp.mean(centred * centred, axis=-1, keepdims=True)
    return centred * lax.rsqrt(spread + NORM_EPS) * gain


def dot(a, b):
    return jnp.dot(a, b, preferred_element_type=F32)


def unit(p, head_mean):
    mean_square = dot((p * p).astype(BF16), head_mean)
    return (p * lax.rsqrt(mean_square + UNIT_EPS)).astype(BF16)


def attend_pair(q, k, v, mask, scale_a, scale_b):
    n = q.shape[0]
    lane = lax.broadcasted_iota(jnp.int32, (1, LANES), 1)
    low = (lane < HEAD).astype(F32).astype(BF16)
    high = (lane >= HEAD).astype(F32).astype(BF16)
    keys = jnp.concatenate([k * low, k * high], axis=0)
    scores = lax.dot_general(q, keys, (((1,), (1,)), ((), ())), preferred_element_type=F32)
    both = lax.broadcasted_iota(jnp.int32, (1, 2 * n), 1)
    factor = jnp.where(both < n, scale_a, scale_b) * (LOG2E / HEAD)
    terms = jnp.exp2(scores * factor) * jnp.concatenate([mask, mask], axis=1)
    values = jnp.concatenate([v * low, v * high], axis=0)
    ones = jnp.concatenate(
        [jnp.broadcast_to(low, (n, LANES)), jnp.broadcast_to(high, (n, LANES))], axis=0
    )
    result = dot(terms.astype(BF16), jnp.concatenate([values, ones], axis=1))
    return (result[:, :LANES] / result[:, LANES:]).astype(BF16)


def kernel(
    sizes,
    atm_ref,
    prev_ref,
    sea_ref,
    ids_ref,
    conv_ref,
    attn_gain_ref,
    qkv_hbm,
    scales_ref,
    out_hbm,
    mlp_gain_ref,
    min_ref,
    mout_ref,
    up_hbm,
    down_hbm,
    flux_ref,
    oconv_ref,
    point_ref,
    ogain_ref,
    oqkv_ref,
    oscale_ref,
    oout_ref,
    return_ref,
    air_ref,
    seaside_ref,
    qkv,
    outw,
    up,
    down,
    cur,
    hrow,
    hcol,
    hcor,
    pad,
    mixed,
    attended,
    same,
    seab,
    start,
    startpad,
    senda,
    recva,
    edges,
    edger,
    opad,
    cpad,
    fine,
    sendb,
    recvb,
    act,
    wsem,
    hsend,
    hrecv,
    asend,
    arecv,
    esend,
    erecv,
    bsend,
    brecv,
):
    n_lat, n_lon, n_comp = sizes
    members, rows, length, width = atm_ref.shape
    blocks = conv_ref.shape[0]
    hidden = up.shape[2]
    piece = length // n_lat
    win = senda.shape[3]
    lats = n_lat * rows
    cells = rows * length
    chunks = width // LANES
    sectors = n_lon * n_comp
    lat = lax.axis_index("lat")
    sector = lax.axis_index("lon") * n_comp + lax.axis_index("comp")

    def place(lat_at, shift):
        at = (sector + shift + sectors) % sectors
        return {"lat": lat_at, "lon": at // n_comp, "comp": at % n_comp}

    copies = [
        pltpu.make_async_copy(source, target, wsem.at[i])
        for i, (source, target) in enumerate(
            ((qkv_hbm, qkv), (out_hbm, outw), (up_hbm, up), (down_hbm, down))
        )
    ]

    barrier = pltpu.get_barrier_semaphore()

    def greet(lat_at, shift):
        pl.semaphore_signal(barrier, inc=1, device_id=place(lat_at, shift), device_id_type=MESH)

    for step in range(1, n_lat):
        greet((lat + step) % n_lat, 0)
    for shift in (-1, 1):
        greet(lat, shift)

        @pl.when(lat > 0)
        def _():
            greet(lat - 1, shift)

        @pl.when(lat < n_lat - 1)
        def _():
            greet(lat + 1, shift)

    @pl.when(lat == 0)
    def _():
        for other in range(n_lat):
            greet(other, -1)

    @pl.when(lat == n_lat - 1)
    def _():
        for other in range(n_lat):
            greet(other, 1)

    for copy in copies:
        copy.start()
    cur[0] = atm_ref[...]

    fixed = n_lat - 1 + 2 + 2

    @pl.when((lat > 0) & (lat < n_lat - 1))
    def _():
        pl.semaphore_wait(barrier, fixed + 4)

    @pl.when((lat == 0) | (lat == n_lat - 1))
    def _():
        pl.semaphore_wait(barrier, fixed + 2)

    def halo(b, m, index):
        dy, dx = SIDES[index]
        source = cur.at[b, m]
        if dy == 0:
            first = 0 if dx < 0 else length - EDGE
            source = source.at[:, pl.ds(first, EDGE)]
            target = hcol.at[b, m, (1 - dx) // 2]
        elif dx == 0:
            source = source.at[0 if dy < 0 else rows - 1]
            target = hrow.at[b, m, (1 - dy) // 2]
        else:
            first = 0 if dx < 0 else length - EDGE
            source = source.at[0 if dy < 0 else rows - 1, pl.ds(first, EDGE)]
            target = hcor.at[b, m, 1 - dy + (1 - dx) // 2]
        return pltpu.make_async_remote_copy(
            src_ref=source,
            dst_ref=target,
            send_sem=hsend.at[b, m, index],
            recv_sem=hrecv.at[b, m, index],
            device_id=place(lat + dy, dx),
            device_id_type=MESH,
        )

    def each_halo(b, m, act_on, receive):
        for index, (dy, dx) in enumerate(SIDES):
            sign = -dy if receive else dy
            if sign < 0:

                @pl.when(lat > 0)
                def _():
                    act_on(halo(b, m, index))
            elif sign > 0:

                @pl.when(lat < n_lat - 1)
                def _():
                    act_on(halo(b, m, index))
            else:
                act_on(halo(b, m, index))

    for m in range(members):
        each_halo(0, m, lambda copy: copy.start(), False)

    pad[0] = jnp.zeros(pad.shape[1:], F32)
    pad[rows + 1] = jnp.zeros(pad.shape[1:], F32)
    opad[...] = jnp.zeros(opad.shape, F32)
    cpad[...] = jnp.zeros(cpad.shape, F32)
    startpad[...] = jnp.zeros(startpad.shape, F32)
    for r in range(rows):
        row = jnp.broadcast_to(ids_ref[r : r + 1, :].astype(F32), (length, length))
        same[r] = (row == row.T).astype(F32)
        row = jnp.broadcast_to(sea_ref[r : r + 1, :].astype(F32), (length, length))
        seab[r * length : (r + 1) * length] = row.T
    head_row = lax.broadcasted_iota(jnp.int32, (LANES, LANES), 0) // HEAD
    head_col = lax.broadcasted_iota(jnp.int32, (LANES, LANES), 1) // HEAD
    head_mean = jnp.where(head_row == head_col, 1.0 / HEAD, 0.0).astype(BF16)

    def piece_copy(m, step):
        to = (lat + step) % n_lat
        return pltpu.make_async_remote_copy(
            src_ref=senda.at[m, to],
            dst_ref=recva.at[m, lat],
            send_sem=asend.at[m, step],
            recv_sem=arecv.at[m, step],
            device_id=place(to, 0),
            device_id_type=MESH,
        )

    def edge_copy(m, side):
        return pltpu.make_async_remote_copy(
            src_ref=edges.at[m, side],
            dst_ref=edger.at[m, lat],
            send_sem=esend.at[m, side],
            recv_sem=erecv.at[m, lat],
            device_id=place(n_lat - 1, -1) if side == 0 else place(0, 1),
            device_id_type=MESH,
        )

    def edge_landed(m, origin):
        return pltpu.make_async_remote_copy(
            src_ref=edges.at[m, 0],
            dst_ref=edger.at[m, origin],
            send_sem=esend.at[m, 0],
            recv_sem=erecv.at[m, origin],
            device_id=place(n_lat - 1, -1),
            device_id_type=MESH,
        )

    def back_copy(m, step):
        to = (lat + step) % n_lat
        return pltpu.make_async_remote_copy(
            src_ref=sendb.at[m, to],
            dst_ref=recvb.at[m, lat],
            send_sem=bsend.at[m, step],
            recv_sem=brecv.at[m, step],
            device_id=place(to, 0),
            device_id_type=MESH,
        )

    def atmosphere(t, carry):
        b = t // members
        m = t % members
        each_halo(b, m, lambda copy: copy.wait_recv(), True)
        pad[1 : rows + 1, RIM : RIM + length] = cur[b, m].astype(F32)
        pad[1 : rows + 1, :RIM] = hcol[b, m, 0].astype(F32)[:, EDGE - RIM :]
        pad[1 : rows + 1, RIM + length :] = hcol[b, m, 1].astype(F32)[:, :RIM]
        for side, at in ((0, 0), (1, rows + 1)):

            @pl.when((lat > 0) if side == 0 else (lat < n_lat - 1))
            def _():
                pad[at, RIM : RIM + length] = hrow[b, m, side].astype(F32)
                pad[at, :RIM] = hcor[b, m, 2 * side].astype(F32)[EDGE - RIM :]
                pad[at, RIM + length :] = hcor[b, m, 2 * side + 1].astype(F32)[:RIM]

        for r in range(rows):
            for c in range(chunks):
                cols = slice(c * LANES, (c + 1) * LANES)
                total = pad[1 + r, RIM : RIM + length, cols]
                for dy in range(3):
                    for dx in range(3):
                        at = RIM - 1 + dx
                        total = (
                            total
                            + pad[r + dy, at : at + length, cols]
                            * conv_ref[b, dy, dx : dx + 1, cols]
                        )
                mixed[r * length : (r + 1) * length, cols] = total.astype(BF16).astype(F32)

        @pl.when(t == 0)
        def _():
            for copy in copies:
                copy.wait()

        normed = layer_norm(mixed[...], attn_gain_ref[pl.ds(b, 1), :]).astype(BF16)
        for c in range(chunks):
            parts = []
            for which in range(3):
                first = which * width + c * LANES
                parts.append(dot(normed, qkv[b, :, first : first + LANES]))
            query = unit(parts[0], head_mean)
            key = unit(parts[1], head_mean)
            value = parts[2].astype(BF16)
            for r in range(rows):
                own = slice(r * length, (r + 1) * length)
                attended[own, c * LANES : (c + 1) * LANES] = attend_pair(
                    query[own],
                    key[own],
                    value[own],
                    same[r],
                    scales_ref[b, 2 * c],
                    scales_ref[b, 2 * c + 1],
                )
        after = (mixed[...] + dot(attended[...], outw[b])).astype(BF16).astype(F32)
        scaled = (
            layer_norm(after, mlp_gain_ref[pl.ds(b, 1), :]) * min_ref[b, pl.ds(m, 1), :]
        ).astype(BF16)
        total = after
        block = 2 * LANES
        for first in range(0, hidden, block):
            lifted = dot(scaled, up[b, :, first : first + block])
            lifted = lifted * mout_ref[b, pl.ds(m, 1), first : first + block]
            total = total + dot(gelu(lifted).astype(BF16), down[b, first : first + block, :])
        result = total.astype(BF16)
        cur[b + 1, m] = result.reshape(rows, length, width)

        @pl.when(b < blocks - 1)
        def _():
            each_halo(b + 1, m, lambda copy: copy.start(), False)

        @pl.when(b == blocks - 1)
        def _():
            final = cur[blocks, m].reshape(cells, width)
            flux = dot(final, flux_ref[...])
            before = prev_ref[m].reshape(cells, LANES).astype(F32)
            begun = (seab[...] * (before + flux)).astype(BF16)
            start[m] = begun
            wide = begun.astype(F32)
            for r in range(rows):
                startpad[r, RIM : RIM + length] = wide[r * length : (r + 1) * length]
                for to in range(n_lat):
                    senda[m, to, r] = startpad[r, to * piece : to * piece + win].astype(BF16)
                edges[m, 0, r] = begun[r * length : r * length + EDGE]
                edges[m, 1, r] = begun[(r + 1) * length - EDGE : (r + 1) * length]
            for step in range(1, n_lat):
                piece_copy(m, step).start()
            for side in range(2):
                edge_copy(m, side).start()
            recva[m, lat] = senda[m, lat]

        return carry

    lax.fori_loop(0, blocks * members, atmosphere, 0)

    fine_cells = lats * win
    half = win // 2
    coarse_cells = fine_cells // 4

    def coarse_of(index):
        return (index // win) // 2 * half + (index % win) // 2

    def nine_taps(ref, which, count, first, wide):
        total = jnp.zeros((count, wide, LANES), F32)
        for dy in range(3):
            for dx in range(3):
                at = first - 1 + dx
                total = (
                    total
                    + ref[dy : dy + count, at : at + wide]
                    * oconv_ref[which, dy, dx : dx + 1, :][None]
                )
        return total.astype(BF16).reshape(count * wide, LANES)

    def ocean(m, carry):
        for step in range(1, n_lat):
            piece_copy(m, step).wait_recv()
        opad[1 : lats + 1, RIM : RIM + win] = (
            recva[m].astype(F32).reshape(lats, win, LANES)
        )

        @pl.when(lat == 0)
        def _():
            for origin in range(n_lat):
                edge_landed(m, origin).wait_recv()
            west = edger[m].astype(F32).reshape(lats, EDGE, LANES)
            opad[1 : lats + 1, RIM : 2 * RIM] = west[:, EDGE - RIM :]

        @pl.when(lat == n_lat - 1)
        def _():
            for origin in range(n_lat):
                edge_landed(m, origin).wait_recv()
            east = edger[m].astype(F32).reshape(lats, EDGE, LANES)
            opad[1 : lats + 1, 2 * RIM + piece : 3 * RIM + piece] = east[:, :RIM]

        first = gelu(dot(nine_taps(opad, 0, lats, RIM, win), point_ref[0])).astype(BF16)
        fine[...] = first
        to_coarse = coarse_of(lax.broadcasted_iota(jnp.int32, (coarse_cells, fine_cells), 1))
        own = lax.broadcasted_iota(jnp.int32, (coarse_cells, fine_cells), 0)
        pooling = jnp.where(to_coarse == own, 0.25, 0.0).astype(BF16)
        pooled = dot(pooling, first).astype(BF16).astype(F32)
        cpad[1 : lats // 2 + 1, RIM : RIM + half] = pooled.reshape(lats // 2, half, LANES)
        second = nine_taps(cpad, 1, lats // 2, RIM, half)
        coarse = gelu(dot(second, point_ref[1])).astype(BF16)
        wide = coarse.astype(F32)
        normed = layer_norm(wide, ogain_ref[...]).astype(BF16)
        projected = dot(normed, oqkv_ref[...])
        column = lax.broadcasted_iota(jnp.int32, (coarse_cells, coarse_cells), 0) % half
        other = lax.broadcasted_iota(jnp.int32, (coarse_cells, coarse_cells), 1) % half
        seen = attend_pair(
            unit(projected[:, :LANES], head_mean),
            unit(projected[:, LANES : 2 * LANES], head_mean),
            projected[:, 2 * LANES :].astype(BF16),
            (column == other).astype(F32),
            oscale_ref[0],
            oscale_ref[1],
        )
        coarse_next = (wide + dot(seen, oout_ref[...])).astype(BF16)
        from_fine = coarse_of(lax.broadcasted_iota(jnp.int32, (fine_cells, coarse_cells), 0))
        own = lax.broadcasted_iota(jnp.int32, (fine_cells, coarse_cells), 1)
        spread = jnp.where(from_fine == own, 1.0, 0.0).astype(BF16)
        merged = (fine[...].astype(F32) + dot(spread, coarse_next)).astype(BF16).astype(F32)
        opad[1 : lats + 1, RIM : RIM + win] = merged.reshape(lats, win, LANES)
        sendb[m] = nine_taps(opad, 2, lats, 2 * RIM, piece).reshape(sendb.shape[1:])
        for step in range(1, n_lat):
            back_copy(m, step).start()
        recvb[m, lat] = sendb[m, lat]
        return carry

    lax.fori_loop(0, members, ocean, 0)

    def finish(m, carry):
        for step in range(1, n_lat):
            back_copy(m, step).wait_recv()
        for origin in range(n_lat):
            landed = recvb[m, origin].astype(F32)
            for r in range(rows):
                at = r * length + origin * piece
                act[at : at + piece] = landed[r * piece : (r + 1) * piece]
        lifted = gelu(dot(act[...].astype(BF16), point_ref[2]))
        sea = seab[...]
        updated = (sea * (start[m].astype(F32) + lifted)).astype(BF16)
        seaside_ref[m] = updated.reshape(rows, length, LANES)
        back = dot(updated, return_ref[...])
        for c in range(chunks):
            cols = slice(c * LANES, (c + 1) * LANES)
            final = cur[blocks, m, :, :, cols].astype(F32).reshape(cells, LANES)
            air = (final + sea * back[:, cols]).astype(BF16)
            air_ref[m, :, :, cols] = air.reshape(rows, length, LANES)
        for step in range(1, n_lat):
            piece_copy(m, step).wait_send()
            back_copy(m, step).wait_send()
        for side in range(2):
            edge_copy(m, side).wait_send()
        for b in range(blocks):
            each_halo(b, m, lambda copy: copy.wait_send(), False)
        return carry

    lax.fori_loop(0, members, finish, 0)


def per_device(sizes, *args):
    atm, prev = args[0], args[1]
    members, rows, length, width = atm.shape
    channels = prev.shape[-1]
    blocks = args[4].shape[0]
    hidden = args[12].shape[2]
    n_lat = sizes[0]
    piece = length // n_lat
    win = -(-(piece + 2 * RIM) // 16) * 16
    lats = rows * n_lat
    args = list(args)
    args[17] = args[17].reshape(1, channels)
    vmem = pl.BlockSpec(memory_space=pltpu.VMEM)
    smem = pl.BlockSpec(memory_space=pltpu.SMEM)
    hbm = pl.BlockSpec(memory_space=pl.ANY)
    specs = [vmem] * len(args)
    for index in (7, 19):
        specs[index] = smem
    for index in (6, 8, 12, 13):
        specs[index] = hbm
    dma = pltpu.SemaphoreType.DMA
    return pl.pallas_call(
        functools.partial(kernel, sizes),
        out_shape=(
            jax.ShapeDtypeStruct(atm.shape, BF16),
            jax.ShapeDtypeStruct(prev.shape, BF16),
        ),
        in_specs=specs,
        out_specs=(vmem, vmem),
        scratch_shapes=[
            pltpu.VMEM(args[6].shape, BF16),
            pltpu.VMEM(args[8].shape, BF16),
            pltpu.VMEM(args[12].shape, BF16),
            pltpu.VMEM(args[13].shape, BF16),
            pltpu.VMEM((blocks + 1,) + atm.shape, BF16),
            pltpu.VMEM((blocks, members, 2, length, width), BF16),
            pltpu.VMEM((blocks, members, 2, rows, EDGE, width), BF16),
            pltpu.VMEM((blocks, members, 4, EDGE, width), BF16),
            pltpu.VMEM((rows + 2, length + 2 * RIM, width), F32),
            pltpu.VMEM((rows * length, width), F32),
            pltpu.VMEM((rows * length, width), BF16),
            pltpu.VMEM((rows, length, length), F32),
            pltpu.VMEM((rows * length, channels), F32),
            pltpu.VMEM((members, rows * length, channels), BF16),
            pltpu.VMEM((rows, length + win, channels), F32),
            pltpu.VMEM((members, n_lat, rows, win, channels), BF16),
            pltpu.VMEM((members, n_lat, rows, win, channels), BF16),
            pltpu.VMEM((members, 2, rows, EDGE, channels), BF16),
            pltpu.VMEM((members, n_lat, rows, EDGE, channels), BF16),
            pltpu.VMEM((lats + 2, win + 2 * RIM, channels), F32),
            pltpu.VMEM((lats // 2 + 2, win // 2 + 2 * RIM, channels), F32),
            pltpu.VMEM((lats * win, channels), BF16),
            pltpu.VMEM((members, n_lat, rows * piece, channels), BF16),
            pltpu.VMEM((members, n_lat, rows * piece, channels), BF16),
            pltpu.VMEM((rows * length, channels), F32),
            dma((4,)),
            dma((blocks, members, len(SIDES))),
            dma((blocks, members, len(SIDES))),
            dma((members, n_lat)),
            dma((members, n_lat)),
            dma((members, 2)),
            dma((members, n_lat)),
            dma((members, n_lat)),
            dma((members, n_lat)),
        ],
        compiler_params=pltpu.CompilerParams(
            collective_id=0, has_side_effects=True, vmem_limit_bytes=48 * 2**20
        ),
        cost_estimate=pl.CostEstimate(
            flops=4 * 10**9, bytes_accessed=10**7, transcendentals=2 * 10**6
        ),
    )(*args)


def solution(mesh):
    sizes = tuple(mesh.shape[axis] for axis in ("lat", "lon", "comp"))
    field = P(None, "lat", ("lon", "comp"), None)
    plane = P("lat", ("lon", "comp"))
    return jax.shard_map(
        functools.partial(per_device, sizes),
        mesh=mesh,
        in_specs=(field, field, plane, plane) + (P(),) * 18,
        out_specs=(field, field),
        check_vma=False,
    )
```

time: 170 us -> 69.8 us (0.41)
  Pallas kernels: 0 us -> 50.6 us
  starting transfers between devices: 36.7 us -> 0 us
  blocking collectives: 26.7 us -> 0 us
  matrix products: 26.2 us -> 0 us
  waiting for transfers between devices: 20.9 us -> 0 us
  other arithmetic: 20.7 us -> 0 us
  local copies, waits for them, and re-layouts: 36 us -> 17.8 us
    pallas_call x0 -> x1, Pallas kernels: none -> 50.6 us  [per_device(): pl.pallas_call(functools.partial(kernel, sizes), out_shape=(jax.ShapeDtyp...]
    ppermute x20 -> x0, starting transfers between devices: 36.7 us -> none  [the longest x12 19.9 us: passed_along(): return lax.ppermute(value, axis, pairs)]
    all_to_all x2 -> x0, blocking collectives: 26.7 us -> none  [the longest x1 14.5 us: per_device(): lax.all_to_all(marine_starting_field, 'lat', split_axis=2, concat_axis=1,...]
    dot_general x21 -> x0, matrix products: 26.2 us -> none  [the longest x2 16.1 us: token_section(): jnp.dot(scaled, up_matrix, preferred_element_type=jnp.float32)]
    mul x23 -> x0, local copies, waits for them, and re-layouts: 24.5 us -> none  [the longest x12 13.6 us: unit_heads(): shaped * lax.rsqrt(jnp.mean(shaped * shaped, axis=-1, keepdims=True) + UN...]
    ppermute x20 -> x0, waiting for transfers between devices: 20.9 us -> none  [the longest x12 9.22 us: passed_along(): return lax.ppermute(value, axis, pairs)]
    unnamed x45 -> x41, local copies, waits for them, and re-layouts: 2.41 us -> 17.8 us
    convert_element_type x16 -> x0, other arithmetic: 8.23 us -> none  [the longest x15 8.23 us: damped_model_field(): return lax.optimization_barrier(values_in.astype(jnp.bfloat16))]
  transfers between devices with their start and end apart: 20 -> 0, of which waited for: 14 -> 0; matrix products, arithmetic and copies ran while one was open for 4% -> 0% of each run, Pallas kernels for 0% -> 0%
where the time goes in v1:
time: 69.8 us; the launch traced here: 69 us
  Pallas kernels  50.6 us (72%)
  local copies, waits for them, and re-layouts  17.8 us (26%)
    pallas_call x1, Pallas kernels, per_device(): pl.pallas_call(functools.partial(kernel, sizes), out_shape=(jax.ShapeDtyp...  50.6 us
    unnamed x41, local copies, waits for them, and re-layouts  17.8 us

profile of v1, /device:TPU:0, one launch (start us, length us, event | category | flops | bytes accessed | tf_op | source)
XLA Modules:
  0.0 69.0 jit_solution(14381732221775780420)
XLA Ops:
  0.6 0.8 %copy.24.conv_ref = f32[2,3,3,384]{3,2,1,0:T(4,128)S(1)} copy(f32[2,3,3,384]{3,0,2,1:T(2,128)} %param.26) | data formatting | bytes 55296 | tf_op args[4]
  1.4 0.0 copy-start
  1.4 1.5 %copy-done = bf16[2,384,1152]{2,1,0:T(8,128)(2,1)S(1)} copy-done((bf16[2,384,1152]{2,1,0:T(8,128)(2,1)S(1)}, bf16[2,384,1152]{2,1,0:T(8,128)(2,1)}, u32[]{:S(2)}) %copy-start) | copy-done | bytes 1769496
  2.9 0.0 copy-start.1
  2.9 1.1 %copy-done.1 = bf16[2,384,384]{2,1,0:T(8,128)(2,1)S(1)} copy-done((bf16[2,384,384]{2,1,0:T(8,128)(2,1)S(1)}, bf16[2,384,384]{2,1,0:T(8,128)(2,1)}, u32[]{:S(2)}) %copy-start.1) | copy-done | bytes 589848
  3.9 0.0 copy-start.2
  3.9 1.0 %copy-done.2 = bf16[2,2,128,384]{3,2,1,0:T(8,128)(2,1)S(1)} copy-done((bf16[2,2,128,384]{3,2,1,0:T(8,128)(2,1)S(1)}, bf16[2,2,128,384]{3,2,1,0:T(8,128)(2,1)}, u32[]{:S(2)}) %copy-start.2) | copy-done | bytes 393240
  4.9 0.0 copy-start.3
  4.9 0.9 %copy-done.3 = bf16[2,2,128,128]{3,2,1,0:T(8,128)(2,1)S(1)} copy-done((bf16[2,2,128,128]{3,2,1,0:T(8,128)(2,1)S(1)}, bf16[2,2,128,128]{3,2,1,0:T(8,128)(2,1)}, u32[]{:S(2)}) %copy-start.3) | copy-done | bytes 131096
  5.8 0.0 copy-start.4
  5.8 0.9 %copy-done.4 = bf16[384,128]{1,0:T(8,128)(2,1)S(1)} copy-done((bf16[384,128]{1,0:T(8,128)(2,1)S(1)}, bf16[384,128]{1,0:T(8,128)(2,1)}, u32[]{:S(2)}) %copy-start.4) | copy-done | bytes 98328
  6.7 0.0 copy-start.5
  6.7 0.9 %copy-done.5 = bf16[3,128,128]{2,1,0:T(8,128)(2,1)S(1)} copy-done((bf16[3,128,128]{2,1,0:T(8,128)(2,1)S(1)}, bf16[3,128,128]{2,1,0:T(8,128)(2,1)}, u32[]{:S(2)}) %copy-start.5) | copy-done | bytes 98328
  7.6 0.0 copy-start.6
  7.6 0.9 %copy-done.6 = bf16[128,384]{1,0:T(8,128)(2,1)S(1)} copy-done((bf16[128,384]{1,0:T(8,128)(2,1)S(1)}, bf16[128,384]{1,0:T(8,128)(2,1)}, u32[]{:S(2)}) %copy-start.6) | copy-done | bytes 98328
  8.5 0.0 copy-start.7
  8.5 0.9 %copy-done.7 = bf16[128,384]{1,0:T(8,128)(2,1)S(1)} copy-done((bf16[128,384]{1,0:T(8,128)(2,1)S(1)}, bf16[128,384]{1,0:T(8,128)(2,1)}, u32[]{:S(2)}) %copy-start.7) | copy-done | bytes 98328
  9.4 0.0 copy-start.8
  9.4 0.8 %copy-done.8 = bf16[128,128]{1,0:T(8,128)(2,1)S(1)} copy-done((bf16[128,128]{1,0:T(8,128)(2,1)S(1)}, bf16[128,128]{1,0:T(8,128)(2,1)}, u32[]{:S(2)}) %copy-start.8) | copy-done | bytes 32792
  10.2 0.0 copy-start.9
  10.2 0.7 %copy-done.9 = f32[2,2,1536]{2,1,0:T(2,128)S(1)} copy-done((f32[2,2,1536]{2,1,0:T(2,128)S(1)}, f32[2,2,1536]{2,1,0:T(2,128)}, u32[]{:S(2)}) %copy-start.9) | copy-done | bytes 24600
  10.9 0.0 copy-start.10
  10.9 0.7 %copy-done.10 = f32[3,3,3,128]{3,2,1,0:T(4,128)S(1)} copy-done((f32[3,3,3,128]{3,2,1,0:T(4,128)S(1)}, f32[3,3,3,128]{3,2,1,0:T(4,128)}, u32[]{:S(2)}) %copy-start.10) | copy-done | bytes 13848
  11.6 0.0 copy-start.11
  11.6 0.7 copy-done.11
  12.3 0.0 copy-start.12
  12.3 0.7 copy-done.12
  13.0 0.0 copy-start.13
  13.0 0.7 copy-done.13
  13.7 0.0 copy-start.14
  13.7 0.7 copy-done.14
  14.4 0.0 copy-start.15
  14.4 0.7 copy-done.15
  15.1 0.0 copy-start.16
  15.1 0.7 copy-done.16
  15.7 0.0 copy-start.17
  15.7 0.7 copy-done.17
  16.4 0.0 copy-start.18
  16.4 0.7 copy-done.18
  17.0 50.6 %shard_map.221 = (bf16[2,2,128,384]{3,2,1,0:T(8,128)(2,1)S(1)}, bf16[2,2,128,128]{3,2,1,0:T(8,128)(2,1)S(1)}) custom-call(bf16[2,2,128,384]{3,2,1,0:T(8,128)(2,1)S(1)} %copy-done.2, bf16[2,2,128,128]{3,2,1,0:T(8,128)(2,1)S(1)} %copy-done.3, s32[2,128]{1,0:T(2,128)S(1)} %copy-done.14, s32[2,128]{1,0:T(2,128)S(1)} %copy-done.15, ...), custom_call_target="tpu_custom_call" | custom-call | flops 4000000000 | bytes 10000000 | tf_op jit(solution)/shard_map/pallas_call | solution.py:506
  67.6 0.7 %copy.27 = bf16[2,2,128,384]{3,2,1,0:T(8,128)(2,1)} copy(bf16[2,2,128,384]{3,2,1,0:T(8,128)(2,1)S(1)} %get-tuple-element.4) | data formatting | bytes 786432
  68.4 0.7 copy.28
Async XLA Ops:
  1.4 1.5 %copy-start = (bf16[2,384,1152]{2,1,0:T(8,128)(2,1)S(1)}, bf16[2,384,1152]{2,1,0:T(8,128)(2,1)}, u32[]{:S(2)}) copy-start(bf16[2,384,1152]{2,1,0:T(8,128)(2,1)} %qkv_hbm.1) | copy-start | bytes 5308420
  2.9 1.1 %copy-start.1 = (bf16[2,384,384]{2,1,0:T(8,128)(2,1)S(1)}, bf16[2,384,384]{2,1,0:T(8,128)(2,1)}, u32[]{:S(2)}) copy-start(bf16[2,384,384]{2,1,0:T(8,128)(2,1)} %out_hbm.1) | copy-start | bytes 1769476
  3.9 1.0 %copy-start.2 = (bf16[2,2,128,384]{3,2,1,0:T(8,128)(2,1)S(1)}, bf16[2,2,128,384]{3,2,1,0:T(8,128)(2,1)}, u32[]{:S(2)}) copy-start(bf16[2,2,128,384]{3,2,1,0:T(8,128)(2,1)} %atm_ref.1) | copy-start | bytes 1179652
  4.9 0.9 %copy-start.3 = (bf16[2,2,128,128]{3,2,1,0:T(8,128)(2,1)S(1)}, bf16[2,2,128,128]{3,2,1,0:T(8,128)(2,1)}, u32[]{:S(2)}) copy-start(bf16[2,2,128,128]{3,2,1,0:T(8,128)(2,1)} %prev_ref.1) | copy-start | bytes 393220
  5.8 0.9 %copy-start.4 = (bf16[384,128]{1,0:T(8,128)(2,1)S(1)}, bf16[384,128]{1,0:T(8,128)(2,1)}, u32[]{:S(2)}) copy-start(bf16[384,128]{1,0:T(8,128)(2,1)} %flux_ref.1) | copy-start | bytes 294916
  6.7 0.9 %copy-start.5 = (bf16[3,128,128]{2,1,0:T(8,128)(2,1)S(1)}, bf16[3,128,128]{2,1,0:T(8,128)(2,1)}, u32[]{:S(2)}) copy-start(bf16[3,128,128]{2,1,0:T(8,128)(2,1)} %point_ref.1) | copy-start | bytes 294916
  7.6 0.9 %copy-start.6 = (bf16[128,384]{1,0:T(8,128)(2,1)S(1)}, bf16[128,384]{1,0:T(8,128)(2,1)}, u32[]{:S(2)}) copy-start(bf16[128,384]{1,0:T(8,128)(2,1)} %oqkv_ref.1) | copy-start | bytes 294916
  8.5 0.9 %copy-start.7 = (bf16[128,384]{1,0:T(8,128)(2,1)S(1)}, bf16[128,384]{1,0:T(8,128)(2,1)}, u32[]{:S(2)}) copy-start(bf16[128,384]{1,0:T(8,128)(2,1)} %return_ref.1) | copy-start | bytes 294916
  9.4 0.8 %copy-start.8 = (bf16[128,128]{1,0:T(8,128)(2,1)S(1)}, bf16[128,128]{1,0:T(8,128)(2,1)}, u32[]{:S(2)}) copy-start(bf16[128,128]{1,0:T(8,128)(2,1)} %oout_ref.1) | copy-start | bytes 98308
  10.2 0.7 %copy-start.9 = (f32[2,2,1536]{2,1,0:T(2,128)S(1)}, f32[2,2,1536]{2,1,0:T(2,128)}, u32[]{:S(2)}) copy-start(f32[2,2,1536]{2,1,0:T(2,128)} %mout_ref.1) | copy-start | bytes 73732
  10.9 0.7 %copy-start.10 = (f32[3,3,3,128]{3,2,1,0:T(4,128)S(1)}, f32[3,3,3,128]{3,2,1,0:T(4,128)}, u32[]{:S(2)}) copy-start(f32[3,3,3,128]{3,2,1,0:T(4,128)} %oconv_ref.1) | copy-start | bytes 41476
  11.6 0.7 %copy-start.11 = (f32[2,2,384]{2,1,0:T(2,128)S(1)}, f32[2,2,384]{2,1,0:T(2,128)}, u32[]{:S(2)}) copy-start(f32[2,2,384]{2,1,0:T(2,128)} %min_ref.1) | copy-start | bytes 18436
  12.3 0.7 copy-start.12
  13.0 0.7 copy-start.13
  13.7 0.7 copy-start.14
  14.4 0.7 copy-start.15
  15.1 0.7 copy-start.16
  15.7 0.7 copy-start.17
  16.4 0.7 copy-start.18

commit v2 on v1

--- a/solution.py
+++ b/solution.py
@@ -20,8 +20,24 @@
 SIDES = [(dy, dx) for dy in (-1, 0, 1) for dx in (-1, 0, 1) if (dy, dx) != (0, 0)]
 
 
+TANH_TERMS = (
+    7.97884216e-01,
+    3.63342834e-02,
+    -3.31299374e-05,
+    -5.52401755e-05,
+    3.96911181e-06,
+    -1.33446555e-07,
+    1.80561970e-09,
+)
+
+
 def gelu(x):
-    return 0.5 * x * (1.0 + lax.erf(x * 0.7071067811865476))
+    square = jnp.minimum(x * x, 36.0)
+    inner = TANH_TERMS[-1]
+    for term in TANH_TERMS[-2::-1]:
+        inner = inner * square + term
+    half = 0.5 * x
+    return half + half * jnp.tanh(x * inner)
 
 
 def layer_norm(x, gain):
@@ -59,20 +75,43 @@
 
 def kernel(
     sizes,
-    atm_ref,
+    atm_hbm,
+    prev_hbm,
+    sea_hbm,
+    ids_hbm,
+    conv_hbm,
+    attn_gain_hbm,
+    qkv_hbm,
+    scales_hbm,
+    out_hbm,
+    mlp_gain_hbm,
+    min_hbm,
+    mout_hbm,
+    up_hbm,
+    down_hbm,
+    flux_hbm,
+    oconv_hbm,
+    point_hbm,
+    ogain_hbm,
+    oqkv_hbm,
+    oscale_hbm,
+    oout_hbm,
+    return_hbm,
+    air_ref,
+    seaside_ref,
     prev_ref,
     sea_ref,
     ids_ref,
     conv_ref,
     attn_gain_ref,
-    qkv_hbm,
+    qkv,
     scales_ref,
-    out_hbm,
+    outw,
     mlp_gain_ref,
     min_ref,
     mout_ref,
-    up_hbm,
-    down_hbm,
+    up,
+    down,
     flux_ref,
     oconv_ref,
     point_ref,
@@ -81,12 +120,6 @@
     oscale_ref,
     oout_ref,
     return_ref,
-    air_ref,
-    seaside_ref,
-    qkv,
-    outw,
-    up,
-    down,
     cur,
     hrow,
     hcol,
@@ -108,6 +141,9 @@
     sendb,
     recvb,
     act,
+    pooling,
+    spread,
+    osame,
     wsem,
     hsend,
     hrecv,
@@ -119,8 +155,8 @@
     brecv,
 ):
     n_lat, n_lon, n_comp = sizes
-    members, rows, length, width = atm_ref.shape
-    blocks = conv_ref.shape[0]
+    members, rows, length, width = atm_hbm.shape
+    blocks = conv_ref.shape[2]
     hidden = up.shape[2]
     piece = length // n_lat
     win = senda.shape[3]
@@ -135,12 +171,37 @@
         at = (sector + shift + sectors) % sectors
         return {"lat": lat_at, "lon": at // n_comp, "comp": at % n_comp}
 
+    pairs = (
+        (atm_hbm, cur.at[0]),
+        (sea_hbm, sea_ref),
+        (ids_hbm, ids_ref),
+        (conv_hbm, conv_ref),
+        (prev_hbm, prev_ref),
+        (attn_gain_hbm, attn_gain_ref),
+        (qkv_hbm, qkv),
+        (scales_hbm, scales_ref),
+        (out_hbm, outw),
+        (mlp_gain_hbm, mlp_gain_ref),
+        (min_hbm, min_ref),
+        (mout_hbm, mout_ref),
+        (up_hbm, up),
+        (down_hbm, down),
+        (flux_hbm, flux_ref),
+        (oconv_hbm, oconv_ref),
+        (point_hbm, point_ref),
+        (ogain_hbm, ogain_ref),
+        (oqkv_hbm, oqkv_ref),
+        (oscale_hbm, oscale_ref),
+        (oout_hbm, oout_ref),
+        (return_hbm, return_ref),
+    )
     copies = [
         pltpu.make_async_copy(source, target, wsem.at[i])
-        for i, (source, target) in enumerate(
-            ((qkv_hbm, qkv), (out_hbm, outw), (up_hbm, up), (down_hbm, down))
-        )
+        for i, (source, target) in enumerate(pairs)
     ]
+    early = 4
+    for copy in copies[:early]:
+        copy.start()
 
     barrier = pltpu.get_barrier_semaphore()
 
@@ -170,9 +231,6 @@
         for other in range(n_lat):
             greet(other, 1)
 
-    for copy in copies:
-        copy.start()
-    cur[0] = atm_ref[...]
 
     fixed = n_lat - 1 + 2 + 2
 
@@ -223,8 +281,12 @@
             else:
                 act_on(halo(b, m, index))
 
-    for m in range(members):
-        each_halo(0, m, lambda copy: copy.start(), False)
+    copies[0].wait()
+    each_halo(0, 0, lambda copy: copy.start(), False)
+    for copy in copies[early:]:
+        copy.start()
+    for copy in copies[1:early]:
+        copy.wait()
 
     pad[0] = jnp.zeros(pad.shape[1:], F32)
     pad[rows + 1] = jnp.zeros(pad.shape[1:], F32)
@@ -240,6 +302,19 @@
     head_col = lax.broadcasted_iota(jnp.int32, (LANES, LANES), 1) // HEAD
     head_mean = jnp.where(head_row == head_col, 1.0 / HEAD, 0.0).astype(BF16)
 
+    fine_cells = lats * win
+    half = win // 2
+    coarse_cells = fine_cells // 4
+    index = lax.broadcasted_iota(jnp.int32, (1, fine_cells), 1)
+    to_coarse = (index // win) // 2 * half + (index % win) // 2
+    own = lax.broadcasted_iota(jnp.int32, (coarse_cells, 1), 0)
+    member_of = jnp.where(own == to_coarse, 1.0, 0.0)
+    pooling[...] = (0.25 * member_of).astype(BF16)
+    spread[...] = member_of.T.astype(BF16)
+    index = lax.broadcasted_iota(jnp.int32, (1, coarse_cells), 1) % half
+    row = jnp.broadcast_to(index.astype(F32), (coarse_cells, coarse_cells))
+    osame[...] = (row == row.T).astype(F32)
+
     def piece_copy(m, step):
         to = (lat + step) % n_lat
         return pltpu.make_async_remote_copy(
@@ -286,6 +361,11 @@
         b = t // members
         m = t % members
         each_halo(b, m, lambda copy: copy.wait_recv(), True)
+
+        @pl.when(t + 1 < members)
+        def _():
+            each_halo(0, t + 1, lambda copy: copy.start(), False)
+
         pad[1 : rows + 1, RIM : RIM + length] = cur[b, m].astype(F32)
         pad[1 : rows + 1, :RIM] = hcol[b, m, 0].astype(F32)[:, EDGE - RIM :]
         pad[1 : rows + 1, RIM + length :] = hcol[b, m, 1].astype(F32)[:, :RIM]
@@ -297,6 +377,7 @@
                 pad[at, :RIM] = hcor[b, m, 2 * side].astype(F32)[EDGE - RIM :]
                 pad[at, RIM + length :] = hcor[b, m, 2 * side + 1].astype(F32)[:RIM]
 
+        taps = [[conv_ref[dy, dx, pl.ds(b, 1), :] for dx in range(3)] for dy in range(3)]
         for r in range(rows):
             for c in range(chunks):
                 cols = slice(c * LANES, (c + 1) * LANES)
@@ -307,21 +388,22 @@
                         total = (
                             total
                             + pad[r + dy, at : at + length, cols]
-                            * conv_ref[b, dy, dx : dx + 1, cols]
+                            * taps[dy][dx][:, cols]
                         )
                 mixed[r * length : (r + 1) * length, cols] = total.astype(BF16).astype(F32)
 
         @pl.when(t == 0)
         def _():
-            for copy in copies:
+            for copy in copies[early:]:
                 copy.wait()
 
         normed = layer_norm(mixed[...], attn_gain_ref[pl.ds(b, 1), :]).astype(BF16)
+        projected = dot(normed, qkv[b])
         for c in range(chunks):
             parts = []
             for which in range(3):
                 first = which * width + c * LANES
-                parts.append(dot(normed, qkv[b, :, first : first + LANES]))
+                parts.append(projected[:, first : first + LANES])
             query = unit(parts[0], head_mean)
             key = unit(parts[1], head_mean)
             value = parts[2].astype(BF16)
@@ -376,24 +458,22 @@
 
     lax.fori_loop(0, blocks * members, atmosphere, 0)
 
-    fine_cells = lats * win
-    half = win // 2
-    coarse_cells = fine_cells // 4
-
-    def coarse_of(index):
-        return (index // win) // 2 * half + (index % win) // 2
-
     def nine_taps(ref, which, count, first, wide):
-        total = jnp.zeros((count, wide, LANES), F32)
-        for dy in range(3):
-            for dx in range(3):
-                at = first - 1 + dx
-                total = (
-                    total
-                    + ref[dy : dy + count, at : at + wide]
-                    * oconv_ref[which, dy, dx : dx + 1, :][None]
-                )
-        return total.astype(BF16).reshape(count * wide, LANES)
+        group = max(1, 128 // wide)
+        parts = []
+        for top in range(0, count, group):
+            size = min(group, count - top)
+            total = None
+            for dy in range(3):
+                for dx in range(3):
+                    at = first - 1 + dx
+                    term = (
+                        ref[top + dy : top + dy + size, at : at + wide]
+                        * oconv_ref[which, dy, dx : dx + 1, :][None]
+                    )
+                    total = term if total is None else total + term
+            parts.append(total.astype(BF16).reshape(size * wide, LANES))
+        return jnp.concatenate(parts, axis=0)
 
     def ocean(m, carry):
         for step in range(1, n_lat):
@@ -418,31 +498,23 @@
 
         first = gelu(dot(nine_taps(opad, 0, lats, RIM, win), point_ref[0])).astype(BF16)
         fine[...] = first
-        to_coarse = coarse_of(lax.broadcasted_iota(jnp.int32, (coarse_cells, fine_cells), 1))
-        own = lax.broadcasted_iota(jnp.int32, (coarse_cells, fine_cells), 0)
-        pooling = jnp.where(to_coarse == own, 0.25, 0.0).astype(BF16)
-        pooled = dot(pooling, first).astype(BF16).astype(F32)
+        pooled = dot(pooling[...], first).astype(BF16).astype(F32)
         cpad[1 : lats // 2 + 1, RIM : RIM + half] = pooled.reshape(lats // 2, half, LANES)
         second = nine_taps(cpad, 1, lats // 2, RIM, half)
         coarse = gelu(dot(second, point_ref[1])).astype(BF16)
         wide = coarse.astype(F32)
         normed = layer_norm(wide, ogain_ref[...]).astype(BF16)
         projected = dot(normed, oqkv_ref[...])
-        column = lax.broadcasted_iota(jnp.int32, (coarse_cells, coarse_cells), 0) % half
-        other = lax.broadcasted_iota(jnp.int32, (coarse_cells, coarse_cells), 1) % half
         seen = attend_pair(
             unit(projected[:, :LANES], head_mean),
             unit(projected[:, LANES : 2 * LANES], head_mean),
             projected[:, 2 * LANES :].astype(BF16),
-            (column == other).astype(F32),
+            osame[...],
             oscale_ref[0],
             oscale_ref[1],
         )
         coarse_next = (wide + dot(seen, oout_ref[...])).astype(BF16)
-        from_fine = coarse_of(lax.broadcasted_iota(jnp.int32, (fine_cells, coarse_cells), 0))
-        own = lax.broadcasted_iota(jnp.int32, (fine_cells, coarse_cells), 1)
-        spread = jnp.where(from_fine == own, 1.0, 0.0).astype(BF16)
-        merged = (fine[...].astype(F32) + dot(spread, coarse_next)).astype(BF16).astype(F32)
+        merged = (fine[...].astype(F32) + dot(spread[...], coarse_next)).astype(BF16).astype(F32)
         opad[1 : lats + 1, RIM : RIM + win] = merged.reshape(lats, win, LANES)
         sendb[m] = nine_taps(opad, 2, lats, 2 * RIM, piece).reshape(sendb.shape[1:])
         for step in range(1, n_lat):
@@ -494,14 +566,13 @@
     lats = rows * n_lat
     args = list(args)
     args[17] = args[17].reshape(1, channels)
+    args[4] = args[4].transpose(1, 2, 0, 3)
     vmem = pl.BlockSpec(memory_space=pltpu.VMEM)
-    smem = pl.BlockSpec(memory_space=pltpu.SMEM)
-    hbm = pl.BlockSpec(memory_space=pl.ANY)
-    specs = [vmem] * len(args)
-    for index in (7, 19):
-        specs[index] = smem
-    for index in (6, 8, 12, 13):
-        specs[index] = hbm
+    specs = [pl.BlockSpec(memory_space=pltpu.HBM)] * len(args)
+    kept = [
+        (pltpu.SMEM if index in (7, 19) else pltpu.VMEM)(arg.shape, arg.dtype)
+        for index, arg in enumerate(args)
+    ]
     dma = pltpu.SemaphoreType.DMA
     return pl.pallas_call(
         functools.partial(kernel, sizes),
@@ -511,11 +582,8 @@
         ),
         in_specs=specs,
         out_specs=(vmem, vmem),
-        scratch_shapes=[
-            pltpu.VMEM(args[6].shape, BF16),
-            pltpu.VMEM(args[8].shape, BF16),
-            pltpu.VMEM(args[12].shape, BF16),
-            pltpu.VMEM(args[13].shape, BF16),
+        scratch_shapes=kept[1:]
+        + [
             pltpu.VMEM((blocks + 1,) + atm.shape, BF16),
             pltpu.VMEM((blocks, members, 2, length, width), BF16),
             pltpu.VMEM((blocks, members, 2, rows, EDGE, width), BF16),
@@ -537,7 +605,10 @@
             pltpu.VMEM((members, n_lat, rows * piece, channels), BF16),
             pltpu.VMEM((members, n_lat, rows * piece, channels), BF16),
             pltpu.VMEM((rows * length, channels), F32),
-            dma((4,)),
+            pltpu.VMEM((lats * win // 4, lats * win), BF16),
+            pltpu.VMEM((lats * win, lats * win // 4), BF16),
+            pltpu.VMEM((lats * win // 4, lats * win // 4), F32),
+            dma((len(args),)),
             dma((blocks, members, len(SIDES))),
             dma((blocks, members, len(SIDES))),
             dma((members, n_lat)),

time: 69.8 us -> 72.1 us (1.033)
  Pallas kernels: 50.6 us -> 52.9 us
    pallas_call x1, Pallas kernels: 50.6 us -> 52.9 us  [per_device(): pl.pallas_call(functools.partial(kernel, sizes), out_shape=(jax.ShapeDtyp...]
    unnamed x41 -> x42, local copies, waits for them, and re-layouts: 17.8 us -> 17.8 us
where the time goes in v2:
time: 72.1 us; the launch traced here: 71.4 us
  Pallas kernels  52.9 us (73%)
  local copies, waits for them, and re-layouts  17.8 us (25%)
    pallas_call x1, Pallas kernels, per_device(): pl.pallas_call(functools.partial(kernel, sizes), out_shape=(jax.ShapeDtyp...  52.9 us
    unnamed x42, local copies, waits for them, and re-layouts  17.8 us

profile of v2, /device:TPU:0, one launch (start us, length us, event | category | flops | bytes accessed | tf_op | source)
XLA Modules:
  0.0 71.4 jit_solution(6376983506032827535)
XLA Ops:
  0.6 0.0 copy-start
  0.6 1.5 %copy-done = bf16[2,384,1152]{2,1,0:T(8,128)(2,1)S(1)} copy-done((bf16[2,384,1152]{2,1,0:T(8,128)(2,1)S(1)}, bf16[2,384,1152]{2,1,0:T(8,128)(2,1)}, u32[]{:S(2)}) %copy-start) | copy-done | bytes 1769496
  2.1 0.0 copy-start.1
  2.1 1.1 %copy-done.1 = bf16[2,384,384]{2,1,0:T(8,128)(2,1)S(1)} copy-done((bf16[2,384,384]{2,1,0:T(8,128)(2,1)S(1)}, bf16[2,384,384]{2,1,0:T(8,128)(2,1)}, u32[]{:S(2)}) %copy-start.1) | copy-done | bytes 589848
  3.2 0.0 copy-start.2
  3.2 1.0 %copy-done.2 = bf16[2,2,128,384]{3,2,1,0:T(8,128)(2,1)S(1)} copy-done((bf16[2,2,128,384]{3,2,1,0:T(8,128)(2,1)S(1)}, bf16[2,2,128,384]{3,2,1,0:T(8,128)(2,1)}, u32[]{:S(2)}) %copy-start.2) | copy-done | bytes 393240
  4.2 0.0 copy-start.3
  4.2 0.9 %copy-done.3 = bf16[2,2,128,128]{3,2,1,0:T(8,128)(2,1)S(1)} copy-done((bf16[2,2,128,128]{3,2,1,0:T(8,128)(2,1)S(1)}, bf16[2,2,128,128]{3,2,1,0:T(8,128)(2,1)}, u32[]{:S(2)}) %copy-start.3) | copy-done | bytes 131096
  5.1 0.0 copy-start.4
  5.1 0.9 %copy-done.4 = bf16[384,128]{1,0:T(8,128)(2,1)S(1)} copy-done((bf16[384,128]{1,0:T(8,128)(2,1)S(1)}, bf16[384,128]{1,0:T(8,128)(2,1)}, u32[]{:S(2)}) %copy-start.4) | copy-done | bytes 98328
  6.0 0.0 copy-start.5
  6.0 0.9 %copy-done.5 = bf16[3,128,128]{2,1,0:T(8,128)(2,1)S(1)} copy-done((bf16[3,128,128]{2,1,0:T(8,128)(2,1)S(1)}, bf16[3,128,128]{2,1,0:T(8,128)(2,1)}, u32[]{:S(2)}) %copy-start.5) | copy-done | bytes 98328
  6.9 0.0 copy-start.6
  6.9 0.9 %copy-done.6 = bf16[128,384]{1,0:T(8,128)(2,1)S(1)} copy-done((bf16[128,384]{1,0:T(8,128)(2,1)S(1)}, bf16[128,384]{1,0:T(8,128)(2,1)}, u32[]{:S(2)}) %copy-start.6) | copy-done | bytes 98328
  7.8 0.0 copy-start.7
  7.8 0.9 %copy-done.7 = bf16[128,384]{1,0:T(8,128)(2,1)S(1)} copy-done((bf16[128,384]{1,0:T(8,128)(2,1)S(1)}, bf16[128,384]{1,0:T(8,128)(2,1)}, u32[]{:S(2)}) %copy-start.7) | copy-done | bytes 98328
  8.7 0.0 copy-start.8
  8.7 0.8 %copy-done.8 = bf16[128,128]{1,0:T(8,128)(2,1)S(1)} copy-done((bf16[128,128]{1,0:T(8,128)(2,1)S(1)}, bf16[128,128]{1,0:T(8,128)(2,1)}, u32[]{:S(2)}) %copy-start.8) | copy-done | bytes 32792
  9.4 0.0 copy-start.9
  9.4 0.7 %copy-done.9 = f32[2,3,3,384]{3,0,2,1:T(2,128)S(1)} copy-done((f32[2,3,3,384]{3,0,2,1:T(2,128)S(1)}, f32[2,3,3,384]{3,0,2,1:T(2,128)}, u32[]{:S(2)}) %copy-start.9) | copy-done | bytes 27672
  10.2 0.0 copy-start.10
  10.2 0.7 %copy-done.10 = f32[2,2,1536]{2,1,0:T(2,128)S(1)} copy-done((f32[2,2,1536]{2,1,0:T(2,128)S(1)}, f32[2,2,1536]{2,1,0:T(2,128)}, u32[]{:S(2)}) %copy-start.10) | copy-done | bytes 24600
  10.9 0.0 copy-start.11
  10.9 0.7 %copy-done.11 = f32[3,3,3,128]{3,2,1,0:T(4,128)S(1)} copy-done((f32[3,3,3,128]{3,2,1,0:T(4,128)S(1)}, f32[3,3,3,128]{3,2,1,0:T(4,128)}, u32[]{:S(2)}) %copy-start.11) | copy-done | bytes 13848
  11.6 0.0 copy-start.12
  11.6 0.7 copy-done.12
  12.3 0.0 copy-start.13
  12.3 0.7 copy-done.13
  13.0 0.0 copy-start.14
  13.0 0.7 copy-done.14
  13.7 0.0 copy-start.15
  13.7 0.7 copy-done.15
  14.4 0.0 copy-start.16
  14.4 0.7 copy-done.16
  15.0 0.0 copy-start.17
  15.0 0.7 copy-done.17
  15.7 0.0 copy-start.18
  15.7 0.7 copy-done.18
  16.4 0.0 copy-start.19
  16.4 0.7 copy-done.19
  17.0 52.9 %shard_map.221 = (bf16[2,2,128,384]{3,2,1,0:T(8,128)(2,1)S(1)}, bf16[2,2,128,128]{3,2,1,0:T(8,128)(2,1)S(1)}) custom-call(bf16[2,2,128,384]{3,2,1,0:T(8,128)(2,1)S(1)} %copy-done.2, bf16[2,2,128,128]{3,2,1,0:T(8,128)(2,1)S(1)} %copy-done.3, s32[2,128]{1,0:T(2,128)S(1)} %copy-done.15, s32[2,128]{1,0:T(2,128)S(1)} %copy-done.16, f32[3,3,2,384]{3,2,1,0:T(2,128)S(1)} %bitcast.2, ...), custom_call_target="tpu_custom_call" | custom-call | flops 4000000000 | bytes 10000000 | tf_op jit(solution)/shard_map/pallas_call | solution.py:577
  70.0 0.7 %copy.26 = bf16[2,2,128,384]{3,2,1,0:T(8,128)(2,1)} copy(bf16[2,2,128,384]{3,2,1,0:T(8,128)(2,1)S(1)} %get-tuple-element.4) | data formatting | bytes 786432
  70.7 0.7 copy.27
Async XLA Ops:
  0.6 1.5 %copy-start = (bf16[2,384,1152]{2,1,0:T(8,128)(2,1)S(1)}, bf16[2,384,1152]{2,1,0:T(8,128)(2,1)}, u32[]{:S(2)}) copy-start(bf16[2,384,1152]{2,1,0:T(8,128)(2,1)} %qkv_hbm.1) | copy-start | bytes 5308420
  2.1 1.1 %copy-start.1 = (bf16[2,384,384]{2,1,0:T(8,128)(2,1)S(1)}, bf16[2,384,384]{2,1,0:T(8,128)(2,1)}, u32[]{:S(2)}) copy-start(bf16[2,384,384]{2,1,0:T(8,128)(2,1)} %out_hbm.1) | copy-start | bytes 1769476
  3.2 1.0 %copy-start.2 = (bf16[2,2,128,384]{3,2,1,0:T(8,128)(2,1)S(1)}, bf16[2,2,128,384]{3,2,1,0:T(8,128)(2,1)}, u32[]{:S(2)}) copy-start(bf16[2,2,128,384]{3,2,1,0:T(8,128)(2,1)} %atm_hbm.1) | copy-start | bytes 1179652
  4.2 0.9 %copy-start.3 = (bf16[2,2,128,128]{3,2,1,0:T(8,128)(2,1)S(1)}, bf16[2,2,128,128]{3,2,1,0:T(8,128)(2,1)}, u32[]{:S(2)}) copy-start(bf16[2,2,128,128]{3,2,1,0:T(8,128)(2,1)} %prev_hbm.1) | copy-start | bytes 393220
  5.1 0.9 %copy-start.4 = (bf16[384,128]{1,0:T(8,128)(2,1)S(1)}, bf16[384,128]{1,0:T(8,128)(2,1)}, u32[]{:S(2)}) copy-start(bf16[384,128]{1,0:T(8,128)(2,1)} %flux_hbm.1) | copy-start | bytes 294916
  6.0 0.9 %copy-start.5 = (bf16[3,128,128]{2,1,0:T(8,128)(2,1)S(1)}, bf16[3,128,128]{2,1,0:T(8,128)(2,1)}, u32[]{:S(2)}) copy-start(bf16[3,128,128]{2,1,0:T(8,128)(2,1)} %point_hbm.1) | copy-start | bytes 294916
  6.9 0.9 %copy-start.6 = (bf16[128,384]{1,0:T(8,128)(2,1)S(1)}, bf16[128,384]{1,0:T(8,128)(2,1)}, u32[]{:S(2)}) copy-start(bf16[128,384]{1,0:T(8,128)(2,1)} %oqkv_hbm.1) | copy-start | bytes 294916
  7.8 0.9 %copy-start.7 = (bf16[128,384]{1,0:T(8,128)(2,1)S(1)}, bf16[128,384]{1,0:T(8,128)(2,1)}, u32[]{:S(2)}) copy-start(bf16[128,384]{1,0:T(8,128)(2,1)} %return_hbm.1) | copy-start | bytes 294916
  8.7 0.8 %copy-start.8 = (bf16[128,128]{1,0:T(8,128)(2,1)S(1)}, bf16[128,128]{1,0:T(8,128)(2,1)}, u32[]{:S(2)}) copy-start(bf16[128,128]{1,0:T(8,128)(2,1)} %oout_hbm.1) | copy-start | bytes 98308
  9.4 0.7 %copy-start.9 = (f32[2,3,3,384]{3,0,2,1:T(2,128)S(1)}, f32[2,3,3,384]{3,0,2,1:T(2,128)}, u32[]{:S(2)}) copy-start(f32[2,3,3,384]{3,0,2,1:T(2,128)} %param.26) | copy-start | bytes 82948
  10.2 0.7 %copy-start.10 = (f32[2,2,1536]{2,1,0:T(2,128)S(1)}, f32[2,2,1536]{2,1,0:T(2,128)}, u32[]{:S(2)}) copy-start(f32[2,2,1536]{2,1,0:T(2,128)} %mout_hbm.1) | copy-start | bytes 73732
  10.9 0.7 %copy-start.11 = (f32[3,3,3,128]{3,2,1,0:T(4,128)S(1)}, f32[3,3,3,128]{3,2,1,0:T(4,128)}, u32[]{:S(2)}) copy-start(f32[3,3,3,128]{3,2,1,0:T(4,128)} %oconv_hbm.1) | copy-start | bytes 41476
  11.6 0.7 copy-start.12
  12.3 0.7 copy-start.13
  13.0 0.7 copy-start.14
  13.7 0.7 copy-start.15
  14.4 0.7 copy-start.16
  15.0 0.7 copy-start.17
  15.7 0.7 copy-start.18
  16.4 0.7 copy-start.19

commit v3 on v2

--- a/solution.py
+++ b/solution.py
@@ -20,24 +20,9 @@
 SIDES = [(dy, dx) for dy in (-1, 0, 1) for dx in (-1, 0, 1) if (dy, dx) != (0, 0)]
 
 
-TANH_TERMS = (
-    7.97884216e-01,
-    3.63342834e-02,
-    -3.31299374e-05,
-    -5.52401755e-05,
-    3.96911181e-06,
-    -1.33446555e-07,
-    1.80561970e-09,
-)
-
-
 def gelu(x):
-    square = jnp.minimum(x * x, 36.0)
-    inner = TANH_TERMS[-1]
-    for term in TANH_TERMS[-2::-1]:
-        inner = inner * square + term
     half = 0.5 * x
-    return half + half * jnp.tanh(x * inner)
+    return half + half * lax.erf(x * 0.7071067811865476)
 
 
 def layer_norm(x, gain):
@@ -144,6 +129,7 @@
     pooling,
     spread,
     osame,
+    active,
     wsem,
     hsend,
     hrecv,
@@ -382,14 +368,13 @@
             for c in range(chunks):
                 cols = slice(c * LANES, (c + 1) * LANES)
                 total = pad[1 + r, RIM : RIM + length, cols]
-                for dy in range(3):
-                    for dx in range(3):
-                        at = RIM - 1 + dx
-                        total = (
-                            total
-                            + pad[r + dy, at : at + length, cols]
-                            * taps[dy][dx][:, cols]
-                        )
+                for dx in range(3):
+                    part = pad[r, :, cols] * taps[0][dx][:, cols]
+                    for dy in range(1, 3):
+                        part = part + pad[r + dy, :, cols] * taps[dy][dx][:, cols]
+                    if dx != 1:
+                        part = pltpu.roll(part, (1 - dx) % part.shape[0], 0)
+                    total = total + part[RIM : RIM + length]
                 mixed[r * length : (r + 1) * length, cols] = total.astype(BF16).astype(F32)
 
         @pl.when(t == 0)
@@ -421,13 +406,12 @@
         scaled = (
             layer_norm(after, mlp_gain_ref[pl.ds(b, 1), :]) * min_ref[b, pl.ds(m, 1), :]
         ).astype(BF16)
-        total = after
         block = 2 * LANES
         for first in range(0, hidden, block):
             lifted = dot(scaled, up[b, :, first : first + block])
             lifted = lifted * mout_ref[b, pl.ds(m, 1), first : first + block]
-            total = total + dot(gelu(lifted).astype(BF16), down[b, first : first + block, :])
-        result = total.astype(BF16)
+            active[:, first : first + block] = gelu(lifted).astype(BF16)
+        result = (after + dot(active[...], down[b])).astype(BF16)
         cur[b + 1, m] = result.reshape(rows, length, width)
 
         @pl.when(b < blocks - 1)
@@ -608,6 +592,7 @@
             pltpu.VMEM((lats * win // 4, lats * win), BF16),
             pltpu.VMEM((lats * win, lats * win // 4), BF16),
             pltpu.VMEM((lats * win // 4, lats * win // 4), F32),
+            pltpu.VMEM((rows * length, hidden), BF16),
             dma((len(args),)),
             dma((blocks, members, len(SIDES))),
             dma((blocks, members, len(SIDES))),
@@ -619,7 +604,7 @@
             dma((members, n_lat)),
         ],
         compiler_params=pltpu.CompilerParams(
-            collective_id=0, has_side_effects=True, vmem_limit_bytes=48 * 2**20
+            collective_id=0, has_side_effects=True, vmem_limit_bytes=64 * 2**20
         ),
         cost_estimate=pl.CostEstimate(
             flops=4 * 10**9, bytes_accessed=10**7, transcendentals=2 * 10**6

time: 72.1 us -> 56.3 us (0.78)
  local copies, waits for them, and re-layouts: 17.8 us -> 3.35 us
  Pallas kernels: 52.9 us -> 52.1 us
    unnamed x42 -> x2, local copies, waits for them, and re-layouts: 17.8 us -> 3.35 us
    pallas_call x1, Pallas kernels: 52.9 us -> 52.1 us  [per_device(): pl.pallas_call(functools.partial(kernel, sizes), out_shape=(jax.ShapeDtyp...]
where the time goes in v3:
time: 56.3 us; the launch traced here: 56.1 us
  Pallas kernels  52.1 us (93%)
  local copies, waits for them, and re-layouts  3.35 us (6%)
  between operations  0.65 us (1%)
    pallas_call x1, Pallas kernels, per_device(): pl.pallas_call(functools.partial(kernel, sizes), out_shape=(jax.ShapeDtyp...  52.1 us
    unnamed x2, local copies, waits for them, and re-layouts  3.35 us

profile of v3, /device:TPU:0, one launch (start us, length us, event | category | flops | bytes accessed | tf_op | source)
XLA Modules:
  0.0 56.1 jit_solution(2299168425839590106)
XLA Ops:
  0.6 52.1 %shard_map.221 = (bf16[2,2,128,384]{3,2,1,0:T(8,128)(2,1)}, bf16[2,2,128,128]{3,2,1,0:T(8,128)(2,1)}) custom-call(bf16[2,2,128,384]{3,2,1,0:T(8,128)(2,1)} %atm_hbm.1, bf16[2,2,128,128]{3,2,1,0:T(8,128)(2,1)} %prev_hbm.1, s32[2,128]{1,0:T(2,128)} %sea_hbm.1, s32[2,128]{1,0:T(2,128)} %ids_hbm.1, f32[3,3,2,384]{3,2,1,0:T(2,128)} %bitcast.2, ...), custom_call_target="tpu_custom_call" | custom-call | flops 4000000000 | bytes 10000000 | tf_op jit(solution)/shard_map/pallas_call | solution.py:561
  52.8 1.8 %copy.26 = bf16[2,2,128,384]{3,2,1,0:T(8,128)(2,1)} copy(bf16[2,2,128,384]{3,2,1,0:T(8,128)(2,1)} %get-tuple-element.4) | data formatting | bytes 786432
  54.5 1.6 %copy.27 = bf16[2,2,128,128]{3,2,1,0:T(8,128)(2,1)} copy(bf16[2,2,128,128]{3,2,1,0:T(8,128)(2,1)} %get-tuple-element.5) | data formatting | bytes 262144
